TPU v7x, 512 devices: a whole 4x4x16 slice. The times are simulated.
512 devices in a mesh: src: 128 (over z, x, core), tgt: 4 (over y).
Axes of the slice: x: 4, y: 4, z: 16, core: 2. Of those that a mesh axis runs over, the one named last changes fastest.
Arguments:
- source_cells: bfloat16 [65536, 256], P('src')
- target_cells: bfloat16 [8192, 256], P('tgt'), may hold values from -6 to 6
- source_mass: float32 [65536], P('src'), may hold values from 0.01 to 10
- target_mass: float32 [8192], P('tgt'), may hold values from 0.01 to 10
- pairs: int32 [128, 4, 32], P('src', 'tgt'), may hold values from 0 to 63, as said below
- counts: int32 [128, 4], P('src', 'tgt'), may hold values from 16 to 32, as said below
Outputs:
- row_potential: float32 [65536], P('src')
- col_potential: float32 [8192], P('tgt')
- mapped: float32 [65536, 256], P('src')
Inputs may be any that keep to these rules, and one draw needn't show every extreme that they name: `pairs`: each entry is a source block times 16 plus a target block of that device; the entries of one device's list are distinct, and its first counts entries name every one of its 4 source blocks and every one of its 16 target blocks. `counts`: some device has 32 live entries.
All inputs are finite; a program needn't handle non-finite values.
Results may differ from a plain program's by a relative error of at most 0.0015.
Values sent between devices are 32-bit elements; how exact they have to be, the bound alone decides.
No kernel may reach another device: no remote copies, remote signals or barrier semaphores. Data moves between devices by JAX's collectives and lax.ppermute only.
A program may use at most 64 MiB of HBM per device.

v0:
```python
import jax
import jax.numpy as jnp
from jax import lax
from jax.sharding import PartitionSpec as P

BLOCK = 128
ITERS = 3
SB_DEV = 4
TB_DEV = 16


entropy = 0.02


def merged_2(x, axis, combine):
    everything = jax.tree.map(lambda part: lax.all_gather(part, axis), x)
    initial = jax.tree.map(lambda part: part[0], everything)

    def hop(k, so_far):
        return combine(so_far, jax.tree.map(lambda part: part[k], everything))

    return lax.fori_loop(1, lax.axis_size(axis), hop, initial)


def group_max(scores, block_ids, group_count, reduce_axis):
    block_max = jnp.max(scores, axis=reduce_axis)
    onehot = block_ids[:, None] == jnp.arange(group_count)[None, :]
    return (jnp.max(jnp.where(onehot[:, :, None], block_max[:, None, :], -jnp.inf), axis=0), onehot)


def fold_blocks(scores, block_ids, group_count, reduce_axis):
    maxima, onehot = group_max(scores, block_ids, group_count, reduce_axis)
    shifted = jnp.expand_dims(maxima[block_ids], reduce_axis)
    partial_value = jnp.sum(jnp.exp(scores - shifted), axis=reduce_axis)
    sumexp = jnp.sum(jnp.where(onehot[:, :, None], partial_value[:, None, :], 0.0), axis=0)
    return (maxima, sumexp)


def combine(first, second):
    merged = jnp.maximum(first[0], second[0])
    return (merged, first[1] * jnp.exp(first[0] - merged) + second[1] * jnp.exp(second[0] - merged))


def shards(source_cells, target_cells, source_mass, target_mass, pairs, counts):
    emb_width = source_cells.shape[1]
    slot_list = pairs.reshape(-1)
    live_count = counts.reshape(())
    row_ids = slot_list // TB_DEV
    col_ids = slot_list % TB_DEV
    is_valid = jnp.arange(slot_list.shape[0]) < live_count
    src_blocks = source_cells.reshape(SB_DEV, BLOCK, emb_width)[row_ids]
    tgt_blocks = target_cells.reshape(TB_DEV, BLOCK, emb_width)[col_ids]
    src_norm = jnp.sum(jnp.square(source_cells.astype(jnp.float32)), axis=-1).reshape(
        SB_DEV, BLOCK
    )[row_ids]
    tgt_norm = jnp.sum(jnp.square(target_cells.astype(jnp.float32)), axis=-1).reshape(
        TB_DEV, BLOCK
    )[col_ids]
    crossed = jnp.einsum("bid,bjd->bij", src_blocks, tgt_blocks, preferred_element_type=jnp.float32)
    stored_costs = (src_norm[:, :, None] + tgt_norm[:, None, :] - 2.0 * crossed) / emb_width

    def costs_now():
        return stored_costs

    source_log = jnp.log(source_mass)
    target_log = jnp.log(target_mass)
    col_pot = jnp.zeros(target_mass.shape, jnp.float32)
    row_pot = jnp.zeros(source_mass.shape, jnp.float32)
    for iteration in range(ITERS):
        block_cost = costs_now()
        potential_block = col_pot.reshape(TB_DEV, BLOCK)[col_ids]
        scores = jnp.where(
            is_valid[:, None, None], (potential_block[:, None, :] - block_cost) / entropy, -jnp.inf
        )
        maxima, sumexp = fold_blocks(scores, row_ids, SB_DEV, 2)
        maxima, sumexp = merged_2((maxima, sumexp), "tgt", combine)
        row_pot = entropy * source_log - entropy * (
            maxima.reshape(-1) + jnp.log(sumexp.reshape(-1))
        )
        block_cost = costs_now()
        potential_block = row_pot.reshape(SB_DEV, BLOCK)[row_ids]
        scores = jnp.where(
            is_valid[:, None, None], (potential_block[:, :, None] - block_cost) / entropy, -jnp.inf
        )
        maxima, sumexp = fold_blocks(scores, col_ids, TB_DEV, 1)
        maxima = maxima.reshape(-1)
        sumexp = sumexp.reshape(-1)
        maxima, sumexp = merged_2((maxima, sumexp), "src", combine)
        col_pot = entropy * target_log - entropy * (maxima + jnp.log(sumexp))
    block_cost = costs_now()
    potential_block = col_pot.reshape(TB_DEV, BLOCK)[col_ids]
    scores = jnp.where(
        is_valid[:, None, None], (potential_block[:, None, :] - block_cost) / entropy, -jnp.inf
    )
    maxima, onehot = group_max(scores, row_ids, SB_DEV, 2)
    peak_value = lax.pmax(maxima.reshape(-1), "tgt").reshape(SB_DEV, BLOCK)
    weights = jnp.exp(scores - peak_value[row_ids][:, :, None]).astype(jnp.bfloat16)
    weight_totals = jnp.sum(weights.astype(jnp.float32), axis=2)
    denominator = jnp.sum(jnp.where(onehot[:, :, None], weight_totals[:, None, :], 0.0), axis=0)
    group_total = slot_list.shape[0] // 8
    weight_groups = weights.reshape(group_total, 8, BLOCK, BLOCK)
    target_groups = tgt_blocks.reshape(group_total, 8, BLOCK, emb_width)
    onehot_groups = onehot.astype(jnp.float32).reshape(group_total, 8, SB_DEV)

    def accumulate(numerator, inputs):
        weight_group, target_group, onehot_group = inputs
        products = jnp.einsum(
            "bij,bjd->bid", weight_group, target_group, preferred_element_type=jnp.float32
        )
        added = jnp.einsum("bk,bid->kid", onehot_group, products, precision=lax.Precision.HIGHEST)
        return (numerator + added, None)

    numerator, unused = lax.scan(
        accumulate,
        jnp.zeros((SB_DEV, BLOCK, emb_width), jnp.float32),
        (weight_groups, target_groups, onehot_groups),
    )
    numerator = numerator.reshape(SB_DEV * BLOCK, emb_width)
    denominator = denominator.reshape(-1)
    numerator, denominator = lax.psum((numerator, denominator), "tgt")
    mapped = numerator / denominator[:, None]
    return (row_pot, col_pot, mapped)


def solution(mesh):
    return jax.shard_map(
        shards,
        mesh=mesh,
        in_specs=(
            P("src", None),
            P("tgt", None),
            P("src"),
            P("tgt"),
            P("src", "tgt", None),
            P("src", "tgt"),
        ),
        out_specs=(P("src"), P("tgt"), P("src", None)),
        check_vma=False,
    )
```

profile of v0, /device:TPU:2, one launch (start us, length us, event | category | flops | bytes accessed | tf_op | source)
XLA Modules:
  0.0 1319.2 jit_solution(9728974561327795490)
XLA Ops:
  9.3 1.6 multiply_reduce_fusion
  11.5 2.0 gather_fusion.4
  14.3 2.0 gather_fusion.3
  16.8 2.9 fusion.16
  20.4 11.2 all-gather.6
  32.6 10.4 all-gather.7
  45.4 1.3 gather_fusion.7
  46.6 1.4 exponential_reduce_fusion.4
  48.9 130.9 %all-gather.25.cloned.1.call-done = f32[128,1,2048]{2,1,0:T(1,128)} async-done(((f32[1,1,2048]{2,1,0:T(1,128)}), f32[128,1,2048]{2,1,0:T(1,128)}) %all-gather.25.cloned.1.call-update) | async-done | bytes 1048592 | tf_op jit(solution)/shard_map/all_gather | solution.py:16
  179.8 1.6 copy.39
  181.4 128.3 %all-gather.27.cloned.1.call-done = f32[128,1,2048]{2,1,0:T(1,128)} async-done(((f32[1,1,2048]{2,1,0:T(1,128)}), f32[128,1,2048]{2,1,0:T(1,128)}) %all-gather.27.cloned.1.call-update) | async-done | bytes 1048592 | tf_op jit(solution)/shard_map/all_gather | solution.py:16
  309.7 2.6 copy.38
  312.3 114.5 %while.114 = (s32[]{:T(128)}, f32[2048]{0:T(1024)S(1)}, f32[2048]{0:T(1024)S(1)}, f32[128,2048]{1,0:T(8,128)S(1)}, f32[128,2048]{1,0:T(8,128)}, /*index=5*/s32[]{:T(128)}, s32[]{:T(128)}, s32[]{:T(128)}) while((s32[]{:T(128)}, f32[2048]{0:T(1024)S(1)}, f32[2048]{0:T(1024)S(1)}, f32[128,2048]{1,0:T(8,128)S(1)}, f32[128,2048]{1,0:T(8,128)}, ...), condition=%wide.region_13.14_spmd, body=%wide.region_12.13_spmd.sunk | while | flops 12293 | bytes 82051 | solution.py:22
  428.9 11.1 all-gather.10
  440.9 10.4 all-gather.11
  453.6 1.3 gather_fusion.11
  454.8 1.4 exponential_reduce_fusion.2
  457.1 122.3 %all-gather.29.cloned.1.call-done = f32[128,1,2048]{2,1,0:T(1,128)} async-done(((f32[1,1,2048]{2,1,0:T(1,128)}), f32[128,1,2048]{2,1,0:T(1,128)}) %all-gather.29.cloned.1.call-update) | async-done | bytes 1048592 | tf_op jit(solution)/shard_map/all_gather | solution.py:16
  579.4 1.6 copy.37
  581.0 128.1 %all-gather.31.cloned.1.call-done = f32[128,1,2048]{2,1,0:T(1,128)} async-done(((f32[1,1,2048]{2,1,0:T(1,128)}), f32[128,1,2048]{2,1,0:T(1,128)}) %all-gather.31.cloned.1.call-update) | async-done | bytes 1048592 | tf_op jit(solution)/shard_map/all_gather | solution.py:16
  709.1 2.6 copy.36
  711.8 114.5 %while.116 = (s32[]{:T(128)}, f32[2048]{0:T(1024)S(1)}, f32[2048]{0:T(1024)S(1)}, f32[128,2048]{1,0:T(8,128)S(1)}, f32[128,2048]{1,0:T(8,128)}, /*index=5*/s32[]{:T(128)}, s32[]{:T(128)}, s32[]{:T(128)}) while((s32[]{:T(128)}, f32[2048]{0:T(1024)S(1)}, f32[2048]{0:T(1024)S(1)}, f32[128,2048]{1,0:T(8,128)S(1)}, f32[128,2048]{1,0:T(8,128)}, ...), condition=%wide.region_25.26_spmd, body=%wide.region_24.25_spmd.sunk | while | flops 12293 | bytes 82051 | solution.py:22
  828.4 11.1 all-gather.14
  840.4 10.4 all-gather.15
  853.0 1.3 gather_fusion.15
  854.3 1.4 exponential_reduce_fusion
  858.0 120.8 %all-gather.33.cloned.1.call-done = f32[128,1,2048]{2,1,0:T(1,128)} async-done(((f32[1,1,2048]{2,1,0:T(1,128)}), f32[128,1,2048]{2,1,0:T(1,128)}) %all-gather.33.cloned.1.call-update) | async-done | bytes 1048592 | tf_op jit(solution)/shard_map/all_gather | solution.py:16
  978.9 2.6 copy.35
  981.5 127.1 %all-gather.35.cloned.1.call-done = f32[128,1,2048]{2,1,0:T(1,128)} async-done(((f32[1,1,2048]{2,1,0:T(1,128)}), f32[128,1,2048]{2,1,0:T(1,128)}) %all-gather.35.cloned.1.call-update) | async-done | bytes 1048592 | tf_op jit(solution)/shard_map/all_gather | solution.py:16
  1108.6 2.6 copy.34
  1111.2 118.6 %while.118 = (s32[]{:T(128)}, f32[2048]{0:T(1024)S(1)}, f32[2048]{0:T(1024)S(1)}, f32[128,2048]{1,0:T(8,128)}, f32[128,2048]{1,0:T(8,128)}, /*index=5*/s32[]{:T(128)}, s32[]{:T(128)}, s32[]{:T(128)}) while((s32[]{:T(128)}, f32[2048]{0:T(1024)S(1)}, f32[2048]{0:T(1024)S(1)}, f32[128,2048]{1,0:T(8,128)}, f32[128,2048]{1,0:T(8,128)}, ...), condition=%wide.region_37.38_spmd, body=%wide.region_36.37_spmd.sunk | while | flops 12293 | bytes 82051 | solution.py:22
  1112.2 0.9 constant_dynamic-slice_fusion.11
  1115.9 0.9 constant_dynamic-slice_fusion.11
  1116.8 0.9 constant_dynamic-slice_fusion.11
  1120.6 0.9 constant_dynamic-slice_fusion.11
  1121.5 0.9 constant_dynamic-slice_fusion.11
  1125.2 0.9 constant_dynamic-slice_fusion.11
  1129.9 0.9 constant_dynamic-slice_fusion.11
  1133.7 0.9 constant_dynamic-slice_fusion.11
  1134.6 0.9 constant_dynamic-slice_fusion.11
  1138.3 0.9 constant_dynamic-slice_fusion.11
  1139.3 0.9 constant_dynamic-slice_fusion.11
  1143.0 0.9 constant_dynamic-slice_fusion.11
  1147.7 0.9 constant_dynamic-slice_fusion.11
  1151.4 0.9 constant_dynamic-slice_fusion.11
  1152.3 0.9 constant_dynamic-slice_fusion.11
  1156.1 0.9 constant_dynamic-slice_fusion.11
  1157.0 0.9 constant_dynamic-slice_fusion.11
  1160.7 0.9 constant_dynamic-slice_fusion.11
  1231.3 10.5 pmax.7
  1242.4 1.7 convert_reduce_fusion
  1244.1 13.3 %while.119 = (s32[]{:T(128)}, f32[4,128,256]{2,0,1:T(4,128)S(1)}, f32[4,8,4]{1,2,0:T(4,128)S(1)}, bf16[4,8,128,128]{2,3,1,0:T(8,128)(2,1)}, bf16[4,8,128,256]{3,2,1,0:T(8,128)(2,1)}, /*index=5*/s32[]{:T(128)}, s32[]{:T(128)}) while((s32[]{:T(128)}, f32[4,128,256]{2,0,1:T(4,128)S(1)}, f32[4,8,4]{1,2,0:T(4,128)S(1)}, ...), condition=%wide.region_42.43_spmd.clone, body=%wide.region_41.42_spmd.clone.sunk | while | flops 79953920 | bytes 3935331 | solution.py:113
  1244.1 1.5 fusion.47
  1245.5 1.8 convolution_add_fusion.2
  1247.4 1.5 fusion.47
  1248.9 1.8 convolution_add_fusion.2
  1250.7 1.5 fusion.47
  1252.2 1.8 convolution_add_fusion.2
  1254.0 1.5 fusion.47
  1255.5 1.8 convolution_add_fusion.2
  1257.4 0.9 copy.18
  1258.4 7.7 psum.15
  1266.1 44.2 %all-reduce.2.cloned.1.call-done = f32[512,256]{1,0:T(8,128)} async-done(((f32[512,256]{1,0:T(8,128)}), f32[512,256]{1,0:T(8,128)}) %all-reduce.2.cloned.1.call-update) | async-done | bytes 524304 | tf_op jit(solution)/shard_map/psum | solution.py:120
  1310.4 2.0 broadcast_divide_fusion
  (858 shorter events, 344.4 us)
Async XLA Ops:
  7.2 4.3 copy-start.1
  7.2 172.6 %all-gather.25.cloned.1.call-start = ((), (), s32[]{:S(2)}) async-start(), calls=%async_computation.1 | async-start | bytes 1056768 | tf_op jit(solution)/shard_map/all_gather | solution.py:16
  11.5 2.6 copy-start
  19.7 23.4 %copy-start.5 = (f32[512]{0:T(512)S(1)}, f32[512]{0:T(512)}, u32[]{:S(2)}) copy-start(f32[512]{0:T(512)} %param.22) | copy-start | bytes 6148
  45.3 264.4 %all-gather.27.cloned.1.call-start = ((), (), s32[]{:S(2)}) async-start(), calls=%async_computation.2 | async-start | bytes 1056768 | tf_op jit(solution)/shard_map/all_gather | solution.py:16
  48.8 530.5 %all-gather.29.cloned.1.call-start = ((), (), s32[]{:S(2)}) async-start(), calls=%async_computation.3 | async-start | bytes 1056768 | tf_op jit(solution)/shard_map/all_gather | solution.py:16
  179.8 132.5 %slice-start.2 = ((f32[128,1,2048]{2,1,0:T(1,128)}), f32[1,1,2048]{2,1,0:T(1,128)S(1)}, s32[]{:S(2)}) async-start(f32[128,1,2048]{2,1,0:T(1,128)} %all-gather.25.cloned.1.call-done), calls=%async_computation.9 | async-start | bytes 16384 | tf_op jit(solution)/shard_map/slice | solution.py:17
  179.8 247.0 %copy-start.4 = (f32[2048]{0:T(1024)S(1)}, f32[2048]{0:T(1024)}, u32[]{:S(2)}) copy-start(f32[2048]{0:T(1024)} %param.23) | copy-start | bytes 24580
  309.7 2.6 slice-start.4
  453.5 255.6 %all-gather.31.cloned.1.call-start = ((), (), s32[]{:S(2)}) async-start(), calls=%async_computation.4 | async-start | bytes 1056768 | tf_op jit(solution)/shard_map/all_gather | solution.py:16
  457.0 521.8 %all-gather.33.cloned.1.call-start = ((), (), s32[]{:S(2)}) async-start(), calls=%async_computation.5 | async-start | bytes 1056768 | tf_op jit(solution)/shard_map/all_gather | solution.py:16
  579.4 132.4 %slice-start.3 = ((f32[128,1,2048]{2,1,0:T(1,128)}), f32[1,1,2048]{2,1,0:T(1,128)S(1)}, s32[]{:S(2)}) async-start(f32[128,1,2048]{2,1,0:T(1,128)} %all-gather.29.cloned.1.call-done), calls=%async_computation.10 | async-start | bytes 16384 | tf_op jit(solution)/shard_map/slice | solution.py:17
  709.1 2.6 slice-start.5
  850.9 4.9 copy-start.2
  851.5 5.8 copy-start.6
  853.0 255.6 %all-gather.35.cloned.1.call-start = ((), (), s32[]{:S(2)}) async-start(), calls=%async_computation.6 | async-start | bytes 1056768 | tf_op jit(solution)/shard_map/all_gather | solution.py:16
  856.5 453.8 %all-reduce.2.cloned.1.call-start = ((), (), s32[]{:S(2)}) async-start(), calls=%async_computation | async-start | bytes 1048576 | tf_op jit(solution)/shard_map/psum | solution.py:120
  978.9 132.4 %slice-start = ((f32[128,1,2048]{2,1,0:T(1,128)}), f32[1,1,2048]{2,1,0:T(1,128)S(1)}, s32[]{:S(2)}) async-start(f32[128,1,2048]{2,1,0:T(1,128)} %all-gather.33.cloned.1.call-done), calls=%async_computation.7 | async-start | bytes 16384 | tf_op jit(solution)/shard_map/slice | solution.py:17
  1108.6 2.6 slice-start.1
  1229.8 14.2 %copy-start.3 = (f32[2048]{0:T(1024)}, f32[2048]{0:T(1024)S(1)}, u32[]{:S(2)}) copy-start(f32[2048]{0:T(1024)S(1)} %multiply_subtract_fusion) | copy-start | bytes 24580
Sparse Core Ops, SparseCore 0:
  45.4 134.3 all-gather.24
  183.3 126.3 all-gather.26
  453.6 125.7 all-gather.28
  582.8 126.3 all-gather.30
  853.1 125.7 all-gather.32
  982.3 126.3 all-gather.34
  1258.4 51.9 all-reduce.1
where the time goes:
time: 1340 us; the launch traced here: 1320 us
  waiting for transfers between devices  802 us (60%)
  local copies, waits for them, and re-layouts  362 us (27%)
  blocking collectives  82.7 us (6%)
  other arithmetic  29.8 us (2%)
  matrix products  16.2 us (1%)
  between operations  15.1 us (1%)
    all_gather x6, waiting for transfers between devices, merged_2(): everything = jax.tree.map(lambda part: lax.all_gather(part, axis), x)  758 us
    dynamic_slice x381, local copies, waits for them, and re-layouts, hop(): return combine(so_far, jax.tree.map(lambda part: part[k], everything))  331 us
    all_gather x6, blocking collectives, merged_2(): everything = jax.tree.map(lambda part: lax.all_gather(part, axis), x)  64.5 us
    psum x1, waiting for transfers between devices, shards(): numerator, denominator = lax.psum((numerator, denominator), 'tgt')  44.2 us
  transfers between devices with their start and end apart: 7, of which 7 were waited for; matrix products, arithmetic and copies ran while one was open for 1% of the time, Pallas kernels for 0%

commit v1 on v0

v1 whole, which is shorter than its diff:
```python
import functools

import jax
import jax.numpy as jnp
from jax import lax
from jax.experimental import pallas as pl
from jax.experimental.pallas import tpu as pltpu
from jax.sharding import Mesh
from jax.sharding import PartitionSpec as P

BLOCK = 128
ITERS = 3
SB = 4
TB = 16
MAXB = 32
E = 256
XC = 8
Z = 16
EPS = 0.02
SRC = ("z", "x", "c")


VMEM = pl.BlockSpec(memory_space=pltpu.VMEM)
SMEM = pl.BlockSpec(memory_space=pltpu.SMEM)


def call(kernel, out_shape, scratch, name, flops=1000000, smem=0, vmem=0):
    return pl.pallas_call(
        kernel,
        out_shape=out_shape,
        in_specs=[SMEM] * smem + [VMEM] * vmem,
        out_specs=jax.tree.map(lambda unused: VMEM, out_shape),
        scratch_shapes=scratch,
        compiler_params=pltpu.CompilerParams(vmem_limit_bytes=16 * 1024 * 1024),
        cost_estimate=pl.CostEstimate(flops=flops, bytes_accessed=2000000, transcendentals=500000),
        name=name,
    )


def f32(*shape):
    return jax.ShapeDtypeStruct(shape, jnp.float32)


def entry(pairs, k):
    value = pairs[k]
    return value >> 4, value & 15


def turned(block):
    return jnp.transpose(block, (1, 0))


def log_sum(parts):
    top = jnp.max(parts, axis=0)
    return top + jnp.log(jnp.sum(jnp.exp(parts - top[None]), axis=0))


def row_peaks(peaks):
    for p in range(SB):
        peaks[p] = jnp.broadcast_to(jnp.max(peaks[p], axis=1, keepdims=True), (BLOCK, BLOCK))


def row_partials(peaks, sums):
    found = []
    for p in range(SB):
        total = jnp.sum(turned(sums[p]), axis=0, keepdims=True)
        found.append(turned(peaks[p])[0:1] + jnp.log(total))
    return jnp.concatenate(found, axis=0)


def cost_kernel(pairs, counts, x, y, cost, partial, x_norm, y_norm, peaks, sums):
    live = counts[0]
    for p in range(SB):
        wide = x[pl.ds(p * BLOCK, BLOCK), :].astype(jnp.float32)
        x_norm[p] = jnp.broadcast_to(jnp.sum(wide * wide, axis=1, keepdims=True), (BLOCK, BLOCK))
    ones = jnp.ones((8, E), jnp.bfloat16)
    dims = (((1,), (1,)), ((), ()))

    def norms(q, unused):
        wide = y[pl.ds(pl.multiple_of(q * BLOCK, BLOCK), BLOCK), :].astype(jnp.float32)
        square = wide * wide
        high = square.astype(jnp.bfloat16)
        low = (square - high.astype(jnp.float32)).astype(jnp.bfloat16)
        y_norm[q] = lax.dot_general(
            ones, high, dims, preferred_element_type=jnp.float32
        ) + lax.dot_general(ones, low, dims, preferred_element_type=jnp.float32)
        return unused

    lax.fori_loop(0, TB, norms, 0)
    peaks[...] = jnp.full(peaks.shape, -jnp.inf, jnp.float32)
    sums[...] = jnp.zeros(sums.shape, jnp.float32)

    def first(k, unused):
        p, q = entry(pairs, k)
        xs = x[pl.ds(pl.multiple_of(p * BLOCK, BLOCK), BLOCK), :]
        ys = y[pl.ds(pl.multiple_of(q * BLOCK, BLOCK), BLOCK), :]
        crossed = lax.dot_general(xs, ys, dims, preferred_element_type=jnp.float32)
        block = (x_norm[p] + y_norm[q][0:1] - 2.0 * crossed) * (1.0 / (E * EPS))
        cost[k] = block
        peaks[p] = jnp.maximum(peaks[p], -block)
        return unused

    lax.fori_loop(0, live, first, 0)
    row_peaks(peaks)

    def second(k, unused):
        p, q = entry(pairs, k)
        sums[p] += jnp.exp(-cost[k] - peaks[p])
        return unused

    lax.fori_loop(0, live, second, 0)
    found = row_partials(peaks, sums)
    for d in range(SB):
        partial[d] = found


def col_kernel(pairs, counts, cost, partials, mass, partial, row_pot, spread, peaks, sums):
    live = counts[0]
    potential = jnp.log(mass[...]) - log_sum(partials[...])
    row_pot[...] = EPS * potential
    for p in range(SB):
        spread[p] = turned(jnp.broadcast_to(potential[p : p + 1], (BLOCK, BLOCK)))
    peaks[...] = jnp.full(peaks.shape, -jnp.inf, jnp.float32)
    sums[...] = jnp.zeros(sums.shape, jnp.float32)

    def first(k, unused):
        p, q = entry(pairs, k)
        score = (spread[p] - cost[k]).reshape(BLOCK // 8, 8, BLOCK)
        peaks[q] = jnp.maximum(peaks[q], jnp.max(score, axis=0))
        return unused

    lax.fori_loop(0, live, first, 0)
    peaks[...] = jnp.broadcast_to(jnp.max(peaks[...], axis=1, keepdims=True), peaks.shape)

    def second(k, unused):
        p, q = entry(pairs, k)
        score = (spread[p] - cost[k]).reshape(BLOCK // 8, 8, BLOCK)
        sums[q] += jnp.sum(jnp.exp(score - peaks[q][None]), axis=0)
        return unused

    lax.fori_loop(0, live, second, 0)
    found = peaks[...][:, 0] + jnp.log(jnp.sum(sums[...], axis=1))
    for d in range(XC):
        partial[d] = found


def merge_kernel(partials, merged):
    found = log_sum(partials[...])
    merged[...] = jnp.broadcast_to(found[None], merged.shape)


def spread_col(partials, mass, spread):
    potential = jnp.log(mass[...]) - log_sum(partials[...])
    for q in range(TB):
        spread[q] = jnp.broadcast_to(potential[q : q + 1], (8, BLOCK))
    return potential


def row_scores(cost, spread, k, q):
    score = spread[q][None] - cost[k].reshape(BLOCK // 8, 8, BLOCK)
    return score.reshape(BLOCK, BLOCK)


def row_passes(pairs, live, cost, spread, peaks, sums, also):
    peaks[...] = jnp.full(peaks.shape, -jnp.inf, jnp.float32)
    sums[...] = jnp.zeros(sums.shape, jnp.float32)

    def first(k, unused):
        p, q = entry(pairs, k)
        peaks[p] = jnp.maximum(peaks[p], row_scores(cost, spread, k, q))
        return unused

    lax.fori_loop(0, live, first, 0)
    row_peaks(peaks)

    def second(k, unused):
        p, q = entry(pairs, k)
        weight = jnp.exp(row_scores(cost, spread, k, q) - peaks[p])
        sums[p] += weight
        also(p, q, weight)
        return unused

    lax.fori_loop(0, live, second, 0)


def row_kernel(pairs, counts, cost, partials, mass, partial, spread, peaks, sums):
    spread_col(partials, mass, spread)
    row_passes(pairs, counts[0], cost, spread, peaks, sums, lambda p, q, weight: None)
    found = row_partials(peaks, sums)
    for d in range(SB):
        partial[d] = found


def map_kernel(pairs, counts, cost, partials, mass, y, packet, col_pot, spread, peaks, sums, total):
    potential = spread_col(partials, mass, spread)
    col_pot[...] = EPS * potential
    total[...] = jnp.zeros(total.shape, jnp.float32)

    def also(p, q, weight):
        ys = y[pl.ds(pl.multiple_of(q * BLOCK, BLOCK), BLOCK), :]
        high = weight.astype(jnp.bfloat16)
        low = (weight - high.astype(jnp.float32)).astype(jnp.bfloat16)
        total[p] += jnp.dot(high, ys, preferred_element_type=jnp.float32) + jnp.dot(
            low, ys, preferred_element_type=jnp.float32
        )

    row_passes(pairs, counts[0], cost, spread, peaks, sums, also)
    found = row_partials(peaks, sums)
    for p in range(SB):
        packet[p, pl.ds(0, BLOCK), :] = total[p] / jnp.sum(sums[p], axis=1, keepdims=True)
        packet[p, pl.ds(BLOCK, 8), :] = jnp.concatenate(
            [jnp.broadcast_to(found[p : p + 1], (8, BLOCK))] * 2, axis=1
        )


def mix_kernel(packets, mapped):
    parts = jnp.concatenate([packets[t, pl.ds(BLOCK, 1), pl.ds(0, BLOCK)] for t in range(SB)])
    share = jnp.exp(parts - jnp.max(parts, axis=0, keepdims=True))
    share = share / jnp.sum(share, axis=0, keepdims=True)
    total = jnp.zeros((BLOCK, E), jnp.float32)
    for t in range(SB):
        factor = turned(jnp.broadcast_to(share[t : t + 1], (BLOCK, BLOCK)))
        total = total + jnp.concatenate([factor, factor], axis=1) * packets[t, pl.ds(0, BLOCK), :]
    mapped[...] = jnp.broadcast_to(total[None], mapped.shape)


def shards(source_cells, target_cells, source_mass, target_mass, pairs, counts):
    pairs = pairs.reshape(MAXB)
    counts = counts.reshape(1)
    source_mass = source_mass.reshape(SB, BLOCK)
    target_mass = target_mass.reshape(TB, BLOCK)
    tall = pltpu.VMEM((SB, BLOCK, BLOCK), jnp.float32)
    flat = pltpu.VMEM((TB, 8, BLOCK), jnp.float32)
    cost, row_part = call(
        cost_kernel,
        (f32(MAXB, BLOCK, BLOCK), f32(SB, SB, BLOCK)),
        [tall, flat, tall, tall],
        "cost",
        smem=2,
        vmem=2,
    )(pairs, counts, source_cells, target_cells)
    for iteration in range(ITERS):
        row_parts = lax.all_to_all(row_part, "t", 0, 0)
        col_part, row_pot = call(
            col_kernel,
            (f32(XC, TB, BLOCK), f32(SB, BLOCK)),
            [tall, flat, flat],
            "cols",
            smem=2,
            vmem=3,
        )(pairs, counts, cost, row_parts, source_mass)
        col_parts = lax.all_to_all(col_part, ("x", "c"), 0, 0)
        col_parts = call(merge_kernel, f32(Z, TB, BLOCK), [], "merge", vmem=1)(col_parts)
        col_parts = lax.all_to_all(col_parts, "z", 0, 0)
        if iteration < ITERS - 1:
            row_part = call(
                row_kernel, f32(SB, SB, BLOCK), [flat, tall, tall], "rows", smem=2, vmem=3
            )(pairs, counts, cost, col_parts, target_mass)
    packet, col_pot = call(
        map_kernel,
        (f32(SB, BLOCK + 8, E), f32(TB, BLOCK)),
        [flat, tall, tall, pltpu.VMEM((SB, BLOCK, E), jnp.float32)],
        "mapping",
        smem=2,
        vmem=4,
    )(pairs, counts, cost, col_parts, target_mass, target_cells)
    packets = lax.all_to_all(packet, "t", 0, 0)
    quarters = call(mix_kernel, f32(SB, BLOCK, E), [], "mix", vmem=1)(packets)
    mapped = lax.all_to_all(quarters, "t", 0, 0)
    return row_pot.reshape(-1), col_pot.reshape(-1), mapped.reshape(SB * BLOCK, E)


def solution(mesh):
    fine = Mesh(mesh.devices.reshape(Z, 4, 2, 4), ("z", "x", "c", "t"))
    return jax.shard_map(
        shards,
        mesh=fine,
        in_specs=(P(SRC, None), P("t", None), P(SRC), P("t"), P(SRC, "t", None), P(SRC, "t")),
        out_specs=(P(SRC), P("t"), P(SRC, None)),
        check_vma=False,
    )
```

time: 1340 us -> 170 us (0.13)
  the two profiles are of different devices: /device:TPU:2 before, /device:TPU:32 now
where the time goes in v1:
time: 170 us; the launch traced here: 169 us
  blocking collectives  140 us (82%)
  Pallas kernels  23.9 us (14%)
  local copies, waits for them, and re-layouts  4.31 us (3%)
    all_to_all x3, blocking collectives, shards(): col_parts = lax.all_to_all(col_parts, 'z', 0, 0)  64.7 us
    all_to_all x3, blocking collectives, shards(): row_parts = lax.all_to_all(row_part, 't', 0, 0)  27.4 us
    all_to_all x3, blocking collectives, shards(): col_parts = lax.all_to_all(col_part, ('x', 'c'), 0, 0)  24.7 us
    all_to_all x1, blocking collectives, shards(): packets = lax.all_to_all(packet, 't', 0, 0)  12.3 us
    all_to_all x1, blocking collectives, shards(): mapped = lax.all_to_all(quarters, 't', 0, 0)  10.5 us
    pallas_call x1, Pallas kernels, shards(): call(cost_kernel, (f32(MAXB, BLOCK, BLOCK), f32(SB, SB, BLOCK)), [tall, f...  7.71 us
    pallas_call x3, Pallas kernels, shards(): call(col_kernel, (f32(XC, TB, BLOCK), f32(SB, BLOCK)), [tall, flat, flat]...  6.85 us
    pallas_call x1, Pallas kernels, shards(): call(map_kernel, (f32(SB, BLOCK + 8, E), f32(TB, BLOCK)), [flat, tall, ta...  5.63 us

profile of v1, /device:TPU:32, one launch (start us, length us, event | category | flops | bytes accessed | tf_op | source)
XLA Modules:
  0.0 169.2 jit_solution(9072323365114560388)
XLA Ops:
  1.3 0.0 copy-start
  1.3 1.2 copy-done
  2.5 0.0 copy-start.1
  2.5 0.9 copy-done.1
  3.5 0.0 copy-start.3
  3.5 0.7 copy-done.3
  4.1 0.0 copy-start.2
  4.1 0.0 copy-start.4
  4.1 7.7 %cost.1 = (f32[32,128,128]{2,1,0:T(8,128)S(1)}, f32[4,4,128]{2,1,0:T(4,128)S(1)}) custom-call(s32[32]{0:T(128)S(1)} %bitcast.17, s32[1]{0:T(128)} %bitcast.7.counts, bf16[512,256]{1,0:T(8,128)(2,1)S(1)} %copy-done.1, bf16[2048,256]{1,0:T(8,128)(2,1)S(1)} %copy-done), custom_call_target="tpu_custom_call" | custom-call | flops 1000000 | bytes 2000000 | tf_op jit(solution)/shard_map/cost/pallas_call | solution.py:234
  11.8 11.1 %all_to_all.55.partials = f32[4,4,128]{2,1,0:T(4,128)S(1)} all-to-all(f32[4,4,128]{2,1,0:T(4,128)S(1)} %get-tuple-element.12), channel_id=1, replica_groups=mesh['z'=16,'x'=4,'c'=2,'t'=4] {'t'}, dimensions={0} | all-to-all | bytes 16384 | tf_op jit(solution)/shard_map/all_to_all | solution.py:243
  22.9 0.0 copy-start.5
  22.9 0.7 copy-done.5
  23.6 2.3 %cols.3 = (f32[8,16,128]{2,1,0:T(8,128)S(1)}, f32[4,128]{1,0:T(4,128)}) custom-call(s32[32]{0:T(128)S(1)} %bitcast.18, s32[1]{0:T(128)} %bitcast.8.counts, f32[32,128,128]{2,1,0:T(8,128)S(1)} %get-tuple-element.11.cost, f32[4,4,128]{2,1,0:T(4,128)S(1)} %all_to_all.55.partials, f32[4,128]{1,0:T(4,128)S(1)} %bitcast.24), custom_call_target="tpu_custom_call" | custom-call | flops 1000000 | bytes 2000000 | tf_op jit(solution)/shard_map/cols/pallas_call | solution.py:244
  25.9 0.0 copy-start.6
  25.9 8.7 %all_to_all.56.partials = f32[8,16,128]{2,1,0:T(8,128)S(1)} all-to-all(f32[8,16,128]{2,1,0:T(8,128)S(1)} %get-tuple-element.13), channel_id=1, replica_groups=mesh['z'=16,'x'=4,'c'=2,'t'=4] {'x','c'}, dimensions={0} | all-to-all | bytes 131072 | tf_op jit(solution)/shard_map/all_to_all | solution.py:252
  34.7 28.4 %all_to_all.57.partials = f32[16,16,128]{2,1,0:T(8,128)S(1)} all-to-all(f32[16,16,128]{2,1,0:T(8,128)S(1)} %merge.3), channel_id=1, replica_groups=mesh['z'=16,'x'=4,'c'=2,'t'=4] {'z'}, dimensions={0} | all-to-all | bytes 262144 | tf_op jit(solution)/shard_map/all_to_all | solution.py:254
  63.1 0.0 copy-done.2
  63.1 0.0 copy-done.4
  63.1 1.7 %rows.2 = f32[4,4,128]{2,1,0:T(4,128)S(1)} custom-call(s32[32]{0:T(128)S(1)} %bitcast.19, s32[1]{0:T(128)} %bitcast.9.counts, f32[32,128,128]{2,1,0:T(8,128)S(1)} %get-tuple-element.11.cost, f32[16,16,128]{2,1,0:T(8,128)S(1)} %all_to_all.57.partials, f32[16,128]{1,0:T(8,128)S(1)} %bitcast.14), custom_call_target="tpu_custom_call" | custom-call | flops 1000000 | bytes 2000000 | tf_op jit(solution)/shard_map/rows/pallas_call | solution.py:256
  64.8 8.1 %all_to_all.58.partials = f32[4,4,128]{2,1,0:T(4,128)S(1)} all-to-all(f32[4,4,128]{2,1,0:T(4,128)S(1)} %rows.2), channel_id=1, replica_groups=mesh['z'=16,'x'=4,'c'=2,'t'=4] {'t'}, dimensions={0} | all-to-all | bytes 16384 | tf_op jit(solution)/shard_map/all_to_all | solution.py:243
  73.0 0.0 copy-done.6
  73.0 2.3 %cols.4 = (f32[8,16,128]{2,1,0:T(8,128)S(1)}, f32[4,128]{1,0:T(4,128)}) custom-call(s32[32]{0:T(128)S(1)} %bitcast.20, s32[1]{0:T(128)} %bitcast.10.counts, f32[32,128,128]{2,1,0:T(8,128)S(1)} %get-tuple-element.11.cost, f32[4,4,128]{2,1,0:T(4,128)S(1)} %all_to_all.58.partials, f32[4,128]{1,0:T(4,128)S(1)} %bitcast.25), custom_call_target="tpu_custom_call" | custom-call | flops 1000000 | bytes 2000000 | tf_op jit(solution)/shard_map/cols/pallas_call | solution.py:244
  75.3 8.0 %all_to_all.59.partials = f32[8,16,128]{2,1,0:T(8,128)S(1)} all-to-all(f32[8,16,128]{2,1,0:T(8,128)S(1)} %get-tuple-element.14), channel_id=1, replica_groups=mesh['z'=16,'x'=4,'c'=2,'t'=4] {'x','c'}, dimensions={0} | all-to-all | bytes 131072 | tf_op jit(solution)/shard_map/all_to_all | solution.py:252
  83.3 18.1 %all_to_all.60.partials = f32[16,16,128]{2,1,0:T(8,128)S(1)} all-to-all(f32[16,16,128]{2,1,0:T(8,128)S(1)} %merge.4), channel_id=1, replica_groups=mesh['z'=16,'x'=4,'c'=2,'t'=4] {'z'}, dimensions={0} | all-to-all | bytes 262144 | tf_op jit(solution)/shard_map/all_to_all | solution.py:254
  101.5 1.7 %rows.3 = f32[4,4,128]{2,1,0:T(4,128)S(1)} custom-call(s32[32]{0:T(128)S(1)} %bitcast.21, s32[1]{0:T(128)} %bitcast.11.counts, f32[32,128,128]{2,1,0:T(8,128)S(1)} %get-tuple-element.11.cost, f32[16,16,128]{2,1,0:T(8,128)S(1)} %all_to_all.60.partials, f32[16,128]{1,0:T(8,128)S(1)} %bitcast.15), custom_call_target="tpu_custom_call" | custom-call | flops 1000000 | bytes 2000000 | tf_op jit(solution)/shard_map/rows/pallas_call | solution.py:256
  103.2 8.1 %all_to_all.61.partials = f32[4,4,128]{2,1,0:T(4,128)S(1)} all-to-all(f32[4,4,128]{2,1,0:T(4,128)S(1)} %rows.3), channel_id=1, replica_groups=mesh['z'=16,'x'=4,'c'=2,'t'=4] {'t'}, dimensions={0} | all-to-all | bytes 16384 | tf_op jit(solution)/shard_map/all_to_all | solution.py:243
  111.3 2.3 %cols.5 = (f32[8,16,128]{2,1,0:T(8,128)S(1)}, f32[4,128]{1,0:T(4,128)}) custom-call(s32[32]{0:T(128)S(1)} %bitcast.22, s32[1]{0:T(128)} %bitcast.12.counts, f32[32,128,128]{2,1,0:T(8,128)S(1)} %get-tuple-element.11.cost, f32[4,4,128]{2,1,0:T(4,128)S(1)} %all_to_all.61.partials, f32[4,128]{1,0:T(4,128)S(1)} %bitcast.26), custom_call_target="tpu_custom_call" | custom-call | flops 1000000 | bytes 2000000 | tf_op jit(solution)/shard_map/cols/pallas_call | solution.py:244
  113.6 8.0 %all_to_all.62.partials = f32[8,16,128]{2,1,0:T(8,128)S(1)} all-to-all(f32[8,16,128]{2,1,0:T(8,128)S(1)} %get-tuple-element.16), channel_id=1, replica_groups=mesh['z'=16,'x'=4,'c'=2,'t'=4] {'x','c'}, dimensions={0} | all-to-all | bytes 131072 | tf_op jit(solution)/shard_map/all_to_all | solution.py:252
  121.6 18.2 %all_to_all.63.partials = f32[16,16,128]{2,1,0:T(8,128)S(1)} all-to-all(f32[16,16,128]{2,1,0:T(8,128)S(1)} %merge.5), channel_id=1, replica_groups=mesh['z'=16,'x'=4,'c'=2,'t'=4] {'z'}, dimensions={0} | all-to-all | bytes 262144 | tf_op jit(solution)/shard_map/all_to_all | solution.py:254
  139.8 5.6 %mapping.1 = (f32[4,136,256]{2,1,0:T(8,128)S(1)}, f32[16,128]{1,0:T(8,128)}) custom-call(s32[32]{0:T(128)S(1)} %bitcast.23, s32[1]{0:T(128)} %bitcast.13.counts, f32[32,128,128]{2,1,0:T(8,128)S(1)} %get-tuple-element.11.cost, f32[16,16,128]{2,1,0:T(8,128)S(1)} %all_to_all.63.partials, f32[16,128]{1,0:T(8,128)S(1)} %bitcast.16, bf16[2048,256]{1,0:T(8,128)(2,1)S(1)} %copy-done), custom_call_target="tpu_custom_call" | custom-call | flops 1000000 | bytes 2000000 | tf_op jit(solution)/shard_map/mapping/pallas_call | solution.py:259
  145.4 12.3 %all_to_all.64.packets = f32[4,136,256]{2,1,0:T(8,128)S(1)} all-to-all(f32[4,136,256]{2,1,0:T(8,128)S(1)} %get-tuple-element.18), channel_id=1, replica_groups=mesh['z'=16,'x'=4,'c'=2,'t'=4] {'t'}, dimensions={0} | all-to-all | bytes 1114112 | tf_op jit(solution)/shard_map/all_to_all | solution.py:267
  157.7 0.2 mix.1
  157.9 10.5 %all_to_all.65 = f32[4,128,256]{2,1,0:T(8,128)S(1)} all-to-all(f32[4,128,256]{2,1,0:T(8,128)S(1)} %mix.1), channel_id=1, replica_groups=mesh['z'=16,'x'=4,'c'=2,'t'=4] {'t'}, dimensions={0} | all-to-all | bytes 1048576 | tf_op jit(solution)/shard_map/all_to_all | solution.py:269
  168.4 0.8 copy.11
  (3 shorter events, 0.1 us)
Async XLA Ops:
  1.3 1.2 copy-start
  2.5 0.9 copy-start.1
  3.5 0.7 copy-start.3
  4.1 59.0 %copy-start.2 = (f32[2048]{0:T(1024)S(1)}, f32[2048]{0:T(1024)}, u32[]{:S(2)}) copy-start(f32[2048]{0:T(1024)} %param.9) | copy-start | bytes 24580
  4.1 59.0 %copy-start.4 = (s32[1,1,32]{2,1,0:T(1,128)S(1)}, s32[1,1,32]{2,1,0:T(1,128)}, u32[]{:S(2)}) copy-start(s32[1,1,32]{2,1,0:T(1,128)} %param.10) | copy-start | bytes 388
  22.9 0.7 copy-start.5
  25.9 47.1 %copy-start.6 = (f32[512]{0:T(512)S(1)}, f32[512]{0:T(512)}, u32[]{:S(2)}) copy-start(f32[512]{0:T(512)} %param.8) | copy-start | bytes 6148

commit v2 on v1

v2 whole, which is shorter than its diff:
```python
import jax
import jax.numpy as jnp
from jax import lax
from jax.experimental import pallas as pl
from jax.experimental.pallas import tpu as pltpu
from jax.sharding import Mesh
from jax.sharding import PartitionSpec as P

BLOCK = 128
ITERS = 3
SB = 4
TB = 16
MAXB = 32
E = 256
XC = 8
Z = 16
EPS = 0.02
SRC = ("z", "x", "c")


VMEM = pl.BlockSpec(memory_space=pltpu.VMEM)
ANY = pl.BlockSpec(memory_space=pl.ANY)
OFFSET = 70.0
LEAST = 1e-28
MOST = 1e37
FIRST_LIMIT = 52


def call(kernel, out_shape, scratch, name, specs, out_specs=None):
    return pl.pallas_call(
        kernel,
        out_shape=out_shape,
        in_specs=specs,
        out_specs=out_specs or jax.tree.map(lambda unused: VMEM, out_shape),
        scratch_shapes=scratch,
        compiler_params=pltpu.CompilerParams(vmem_limit_bytes=16 * 1024 * 1024),
        cost_estimate=pl.CostEstimate(flops=1000000, bytes_accessed=2000000, transcendentals=500000),
        name=name,
    )


def f32(*shape):
    return jax.ShapeDtypeStruct(shape, jnp.float32)


def fetch(pairs_hbm, counts_hbm, pairs, counts, done):
    copies = [
        pltpu.make_async_copy(pairs_hbm, pairs, done.at[0]),
        pltpu.make_async_copy(counts_hbm, counts, done.at[1]),
    ]
    for copy in copies:
        copy.start()
    return copies


def fetched(copies, counts):
    for copy in copies:
        copy.wait()
    return counts[0]


def entry(pairs, k):
    value = pairs[k]
    return value >> 4, value & 15


def turned(block):
    return jnp.transpose(block, (1, 0))


def log_sum(parts):
    top = jnp.max(parts, axis=0)
    return top + jnp.log(jnp.sum(jnp.exp(parts - top[None]), axis=0))


def in_range(totals):
    return jnp.logical_and(jnp.min(totals) >= LEAST, jnp.max(totals) <= MOST)


def spread_rows(potential, spread):
    for p in range(SB):
        spread[p] = turned(jnp.broadcast_to(potential[p : p + 1], (BLOCK, BLOCK)))


def spread_cols(potential, spread):
    for q in range(TB):
        spread[q] = jnp.broadcast_to(potential[q : q + 1], (8, BLOCK))


def row_scores(gram, spread, p, q):
    score = spread[q][None] + gram[p, q].reshape(BLOCK // 8, 8, BLOCK)
    return score.reshape(BLOCK, BLOCK)


def row_totals(sums):
    return jnp.concatenate(
        [jnp.sum(turned(sums[p]), axis=0, keepdims=True) for p in range(SB)], axis=0
    )


def row_passes(pairs, live, gram, spread, peaks, sums, found, also):
    peaks[...] = jnp.full(peaks.shape, -jnp.inf, jnp.float32)
    sums[...] = jnp.zeros(sums.shape, jnp.float32)

    def first(k, unused):
        p, q = entry(pairs, k)
        peaks[p] = jnp.maximum(peaks[p], row_scores(gram, spread, p, q))
        return unused

    lax.fori_loop(0, live, first, 0)
    for p in range(SB):
        peaks[p] = jnp.broadcast_to(jnp.max(peaks[p], axis=1, keepdims=True), (BLOCK, BLOCK))

    def second(k, unused):
        p, q = entry(pairs, k)
        weight = jnp.exp(row_scores(gram, spread, p, q) - peaks[p])
        sums[p] += weight
        also(p, q, weight)
        return unused

    lax.fori_loop(0, live, second, 0)
    tops = jnp.concatenate([turned(peaks[p])[0:1] for p in range(SB)], axis=0)
    found[...] = tops + jnp.log(row_totals(sums))


def row_pass(pairs, live, gram, spread, before, row_spread, sums, found, peaks, also):
    sums[...] = jnp.zeros(sums.shape, jnp.float32)

    def only(k, unused):
        p, q = entry(pairs, k)
        weight = jnp.exp(row_scores(gram, spread, p, q) + row_spread[p])
        sums[p] += weight
        also(p, q, weight)
        return unused

    lax.fori_loop(0, live, only, 0)
    totals = row_totals(sums)
    found[...] = jnp.log(totals) - (before + OFFSET)

    @pl.when(jnp.logical_not(in_range(totals)))
    def again():
        row_passes(pairs, live, gram, spread, peaks, sums, found, also)


def folded(cells):
    wide = cells.astype(jnp.float32)
    square = wide * wide
    square = turned(square[:, :BLOCK] + square[:, BLOCK:])
    return jnp.sum(square, axis=0, keepdims=True) * (1.0 / (E * EPS))


def nothing(p, q, weight):
    return None


def gram_kernel(
    pairs_hbm,
    counts_hbm,
    x,
    y,
    gram,
    partial,
    x_norm,
    y_norm,
    pairs,
    counts,
    done,
    spread,
    row_spread,
    peaks,
    sums,
    found,
):
    lists = fetch(pairs_hbm, counts_hbm, pairs, counts, done)
    for p in range(SB):
        x_norm[pl.ds(p, 1)] = folded(x[pl.ds(p * BLOCK, BLOCK), :])

    def chunk(c, unused):
        cells = y[pl.ds(pl.multiple_of(c * 2 * BLOCK, 2 * BLOCK), 2 * BLOCK), :]
        dims = (((1,), (1,)), ((), ()))
        crossed = lax.dot_general(x[...], cells, dims, preferred_element_type=jnp.float32)
        crossed = crossed * (2.0 / (E * EPS))
        for half in range(2):
            norm = folded(cells[half * BLOCK : (half + 1) * BLOCK])
            spread[2 * c + half] = jnp.broadcast_to(-norm, (8, BLOCK))
            for p in range(SB):
                gram[p, 2 * c + half] = crossed[
                    p * BLOCK : (p + 1) * BLOCK, half * BLOCK : (half + 1) * BLOCK
                ]
        return unused

    lax.fori_loop(0, TB // 2, chunk, 0)
    y_norm[...] = -spread[...][:, 0]
    before = -x_norm[...]
    spread_rows(before + OFFSET, row_spread)
    live = fetched(lists, counts)
    row_pass(pairs, live, gram, spread, before, row_spread, sums, found, peaks, nothing)
    for d in range(SB):
        partial[d] = found[...]


def col_kernel(
    pairs_hbm,
    counts_hbm,
    gram,
    partials,
    mass,
    before,
    partial,
    potential,
    pairs,
    counts,
    done,
    spread,
    col_spread,
    peaks,
    sums,
    found,
):
    lists = fetch(pairs_hbm, counts_hbm, pairs, counts, done)
    potential[...] = jnp.log(mass[...]) - log_sum(partials[...])
    spread_rows(potential[...], spread)
    spread_cols(before[...] + OFFSET, col_spread)
    sums[...] = jnp.zeros(sums.shape, jnp.float32)
    live = fetched(lists, counts)

    def scores(p, q):
        return (spread[p] + gram[p, q]).reshape(BLOCK // 8, 8, BLOCK)

    def only(k, unused):
        p, q = entry(pairs, k)
        sums[q] += jnp.sum(jnp.exp(scores(p, q) + col_spread[q][None]), axis=0)
        return unused

    lax.fori_loop(0, live, only, 0)
    totals = jnp.sum(sums[...], axis=1)
    found[...] = jnp.log(totals) - (before[...] + OFFSET)

    @pl.when(jnp.logical_not(in_range(totals)))
    def again():
        peaks[...] = jnp.full(peaks.shape, -jnp.inf, jnp.float32)
        sums[...] = jnp.zeros(sums.shape, jnp.float32)

        def first(k, unused):
            p, q = entry(pairs, k)
            peaks[q] = jnp.maximum(peaks[q], jnp.max(scores(p, q), axis=0))
            return unused

        lax.fori_loop(0, live, first, 0)
        peaks[...] = jnp.broadcast_to(jnp.max(peaks[...], axis=1, keepdims=True), peaks.shape)

        def second(k, unused):
            p, q = entry(pairs, k)
            sums[q] += jnp.sum(jnp.exp(scores(p, q) - peaks[q][None]), axis=0)
            return unused

        lax.fori_loop(0, live, second, 0)
        found[...] = peaks[...][:, 0] + jnp.log(jnp.sum(sums[...], axis=1))

    for d in range(XC):
        partial[d] = found[...]


def merge_kernel(partials, merged):
    found = log_sum(partials[...])
    merged[...] = jnp.broadcast_to(found[None], merged.shape)


def row_kernel(
    pairs_hbm,
    counts_hbm,
    gram,
    partials,
    mass,
    before,
    partial,
    potential,
    pairs,
    counts,
    done,
    spread,
    row_spread,
    peaks,
    sums,
    found,
):
    lists = fetch(pairs_hbm, counts_hbm, pairs, counts, done)
    potential[...] = jnp.log(mass[...]) - log_sum(partials[...])
    spread_cols(potential[...], spread)
    spread_rows(before[...] + OFFSET, row_spread)
    live = fetched(lists, counts)
    row_pass(
        pairs, live, gram, spread, before[...], row_spread, sums, found, peaks, nothing
    )
    for d in range(SB):
        partial[d] = found[...]


def map_kernel(
    pairs_hbm,
    counts_hbm,
    gram,
    partials,
    mass,
    before,
    x_norm,
    y_norm,
    y,
    packet,
    row_pot,
    col_pot,
    pairs,
    counts,
    done,
    spread,
    row_spread,
    peaks,
    sums,
    found,
    high,
    low,
    rows_out,
    cols_out,
):
    lists = fetch(pairs_hbm, counts_hbm, pairs, counts, done)
    potential = jnp.log(mass[...]) - log_sum(partials[...])
    rows_out[...] = EPS * (before[...] + x_norm[...])
    cols_out[...] = EPS * (potential + y_norm[...])
    copies = [
        pltpu.make_async_copy(rows_out, row_pot, done.at[2]),
        pltpu.make_async_copy(cols_out, col_pot, done.at[3]),
    ]
    for copy in copies:
        copy.start()
    spread_cols(potential, spread)
    spread_rows(before[...] + OFFSET, row_spread)
    high[...] = jnp.zeros(high.shape, jnp.bfloat16)
    low[...] = jnp.zeros(low.shape, jnp.bfloat16)

    def also(p, q, weight):
        rows = pl.ds(pl.multiple_of(p * BLOCK, BLOCK), BLOCK)
        cols = pl.ds(pl.multiple_of(q * BLOCK, BLOCK), BLOCK)
        leading = weight.astype(jnp.bfloat16)
        high[rows, cols] = leading
        low[rows, cols] = (weight - leading.astype(jnp.float32)).astype(jnp.bfloat16)

    live = fetched(lists, counts)
    row_pass(pairs, live, gram, spread, before[...], row_spread, sums, found, peaks, also)
    total = jnp.dot(high[...], y[...], preferred_element_type=jnp.float32) + jnp.dot(
        low[...], y[...], preferred_element_type=jnp.float32
    )
    for p in range(SB):
        packet[p, pl.ds(0, BLOCK), :] = total[p * BLOCK : (p + 1) * BLOCK] / jnp.sum(
            sums[p], axis=1, keepdims=True
        )
        packet[p, pl.ds(BLOCK, 8), :] = jnp.concatenate(
            [jnp.broadcast_to(found[pl.ds(p, 1)], (8, BLOCK))] * 2, axis=1
        )
    for copy in copies:
        copy.wait()


def mix_kernel(packets, mapped):
    parts = jnp.concatenate([packets[t, pl.ds(BLOCK, 1), pl.ds(0, BLOCK)] for t in range(SB)])
    share = jnp.exp(parts - jnp.max(parts, axis=0, keepdims=True))
    share = share / jnp.sum(share, axis=0, keepdims=True)
    total = jnp.zeros((BLOCK, E), jnp.float32)
    for t in range(SB):
        factor = turned(jnp.broadcast_to(share[t : t + 1], (BLOCK, BLOCK)))
        total = total + jnp.concatenate([factor, factor], axis=1) * packets[t, pl.ds(0, BLOCK), :]
    mapped[...] = jnp.broadcast_to(total[None], mapped.shape)


def shards(source_cells, target_cells, source_mass, target_mass, pairs, counts):
    pairs = pairs.reshape(MAXB)
    counts = counts.reshape(1)
    source_mass = source_mass.reshape(SB, BLOCK)
    target_mass = target_mass.reshape(TB, BLOCK)
    tall = pltpu.VMEM((SB, BLOCK, BLOCK), jnp.float32)
    flat = pltpu.VMEM((TB, 8, BLOCK), jnp.float32)
    rows = pltpu.VMEM((SB, BLOCK), jnp.float32)
    cols = pltpu.VMEM((TB, BLOCK), jnp.float32)
    dense = pltpu.VMEM((SB * BLOCK, TB * BLOCK), jnp.bfloat16)
    lists = [pltpu.SMEM((MAXB,), jnp.int32), pltpu.SMEM((1,), jnp.int32)]

    def sems(count):
        return pltpu.SemaphoreType.DMA((count,))

    gram, row_part, x_norm, y_norm = call(
        gram_kernel,
        (f32(SB, TB, BLOCK, BLOCK), f32(SB, SB, BLOCK), f32(SB, BLOCK), f32(TB, BLOCK)),
        lists + [sems(2), flat, tall, tall, tall, rows],
        "gram",
        [ANY] * 2 + [VMEM] * 2,
    )(pairs, counts, source_cells, target_cells)
    col_pot = -y_norm
    for iteration in range(ITERS):
        row_parts = lax.all_to_all(row_part, "t", 0, 0)
        col_part, row_pot = call(
            col_kernel,
            (f32(XC, TB, BLOCK), f32(SB, BLOCK)),
            lists + [sems(2), tall, flat, flat, flat, cols],
            "cols",
            [ANY] * 2 + [VMEM] * 4,
        )(pairs, counts, gram, row_parts, source_mass, col_pot)
        col_parts = lax.all_to_all(col_part, ("x", "c"), 0, 0)
        col_parts = call(merge_kernel, f32(Z, TB, BLOCK), [], "merge", [VMEM])(col_parts)
        col_parts = lax.all_to_all(col_parts, "z", 0, 0)
        if iteration < ITERS - 1:
            row_part, col_pot = call(
                row_kernel,
                (f32(SB, SB, BLOCK), f32(TB, BLOCK)),
                lists + [sems(2), flat, tall, tall, tall, rows],
                "rows",
                [ANY] * 2 + [VMEM] * 4,
            )(pairs, counts, gram, col_parts, target_mass, row_pot)
    packet, row_pot, col_pot = call(
        map_kernel,
        (f32(SB, BLOCK + 8, E), f32(SB, BLOCK), f32(TB, BLOCK)),
        lists + [sems(4), flat, tall, tall, tall, rows, dense, dense, rows, cols],
        "mapping",
        [ANY] * 2 + [VMEM] * 7,
        out_specs=(VMEM, ANY, ANY),
    )(pairs, counts, gram, col_parts, target_mass, row_pot, x_norm, y_norm, target_cells)
    packets = lax.all_to_all(packet, "t", 0, 0)
    quarters = call(mix_kernel, f32(SB, BLOCK, E), [], "mix", [VMEM])(packets)
    mapped = lax.all_to_all(quarters, "t", 0, 0)
    return row_pot.reshape(-1), col_pot.reshape(-1), mapped.reshape(SB * BLOCK, E)


def solution(mesh):
    fine = Mesh(mesh.devices.reshape(Z, 4, 2, 4), ("z", "x", "c", "t"))
    return jax.shard_map(
        shards,
        mesh=fine,
        in_specs=(P(SRC, None), P("t", None), P(SRC), P("t"), P(SRC, "t", None), P(SRC, "t")),
        out_specs=(P(SRC), P("t"), P(SRC, None)),
        check_vma=False,
    )
```

time: 170 us -> 164 us (0.965)
  the two profiles are of different devices: /device:TPU:32 before, /device:TPU:2 now
where the time goes in v2:
time: 164 us
  blocking collectives  128 us (78%)
  Pallas kernels  15.9 us (10%)
  local copies, waits for them, and re-layouts  9.1 us (6%)
  waiting for transfers between devices  5.32 us (3%)
  starting transfers between devices  4.33 us (3%)
    all_to_all x3, blocking collectives, shards(): col_parts = lax.all_to_all(col_parts, 'z', 0, 0)  63.7 us
    all_to_all x3, blocking collectives, shards(): col_parts = lax.all_to_all(col_part, ('x', 'c'), 0, 0)  26.6 us
    all_to_all x2, blocking collectives, shards(): row_parts = lax.all_to_all(row_part, 't', 0, 0)  15.9 us
    all_to_all x1, blocking collectives, shards(): packets = lax.all_to_all(packet, 't', 0, 0)  10.9 us
    all_to_all x1, blocking collectives, shards(): mapped = lax.all_to_all(quarters, 't', 0, 0)  10.5 us
    unnamed x25, local copies, waits for them, and re-layouts  9.1 us
    all_to_all x1, waiting for transfers between devices, shards(): row_parts = lax.all_to_all(row_part, 't', 0, 0)  5.32 us
    pallas_call x1, Pallas kernels, shards(): call(gram_kernel, (f32(SB, TB, BLOCK, BLOCK), f32(SB, SB, BLOCK), f32(SB,...  5.27 us
  transfers between devices with their start and end apart: 1, of which 1 were waited for; matrix products, arithmetic and copies ran while one was open for 0% of the time, Pallas kernels for 0%

profile of v2, /device:TPU:2, one launch (start us, length us, event | category | flops | bytes accessed | tf_op | source)
XLA Modules:
  0.0 163.7 jit_solution(8523625757020906633)
XLA Ops:
  1.3 0.0 copy-start.3
  1.3 1.2 copy-done.3
  2.5 0.0 copy-start.5
  2.5 0.9 copy-done.5
  3.5 0.0 copy-start.7
  3.5 0.7 copy-done.7
  4.1 0.0 copy-start.6
  4.1 5.3 %gram.1 = (f32[4,16,128,128]{3,2,1,0:T(8,128)S(1)}, f32[4,4,128]{2,1,0:T(4,128)}, f32[4,128]{1,0:T(4,128)S(1)}, f32[16,128]{1,0:T(8,128)S(1)}) custom-call(s32[32]{0:T(128)S(1)} %bitcast.17, s32[1]{0:T(128)} %bitcast.7.counts_hbm, bf16[512,256]{1,0:T(8,128)(2,1)S(1)} %copy-done.5, bf16[2048,256]{1,0:T(8,128)(2,1)S(1)} %copy-done.3), custom_call_target="tpu_custom_call" | custom-call | flops 1000000 | bytes 2000000 | tf_op jit(solution)/shard_map/gram/pallas_call | solution.py:389
  9.4 0.0 copy-start
  9.4 1.9 %copy-done = f32[4,16,128,128]{3,2,1,0:T(8,128)} copy-done((f32[4,16,128,128]{3,2,1,0:T(8,128)}, f32[4,16,128,128]{3,2,1,0:T(8,128)S(1)}, u32[]{:S(2)}) %copy-start) | copy-done | bytes 4194328
  11.3 4.3 %all-to-all-start = ((f32[4,4,128]{2,1,0:T(4,128)}), f32[4,4,128]{2,1,0:T(4,128)S(1)}, u32[]{:S(2)}, u32[]{:S(2)}) async-start(f32[4,4,128]{2,1,0:T(4,128)} %get-tuple-element.21), calls=%async_computation | async-start | bytes 16384 | tf_op jit(solution)/shard_map/all_to_all | solution.py:398
  15.7 5.3 %all-to-all-done.partials = f32[4,4,128]{2,1,0:T(4,128)S(1)} async-done(((f32[4,4,128]{2,1,0:T(4,128)}), f32[4,4,128]{2,1,0:T(4,128)S(1)}, u32[]{:S(2)}, u32[]{:S(2)}) %all-to-all-start) | async-done | bytes 8224 | tf_op jit(solution)/shard_map/all_to_all | solution.py:398
  21.0 0.0 copy-start.1
  21.0 2.2 %copy-done.1 = f32[4,16,128,128]{3,2,1,0:T(8,128)S(1)} copy-done((f32[4,16,128,128]{3,2,1,0:T(8,128)S(1)}, f32[4,16,128,128]{3,2,1,0:T(8,128)}, u32[]{:S(2)}) %copy-start.1) | copy-done | bytes 4194328
  23.2 0.0 copy-start.8
  23.2 0.7 copy-done.8
  23.8 0.0 copy-start.10
  23.8 0.7 copy-done.10
  24.5 0.0 copy-start.2
  24.5 0.0 copy-start.11
  24.5 1.5 cols.3
  26.0 10.9 %all_to_all.55.partials = f32[8,16,128]{2,1,0:T(8,128)S(1)} all-to-all(f32[8,16,128]{2,1,0:T(8,128)S(1)} %get-tuple-element.23), channel_id=1, replica_groups=mesh['z'=16,'x'=4,'c'=2,'t'=4] {'x','c'}, dimensions={0} | all-to-all | bytes 131072 | tf_op jit(solution)/shard_map/all_to_all | solution.py:406
  37.0 27.0 %all_to_all.56.partials = f32[16,16,128]{2,1,0:T(8,128)S(1)} all-to-all(f32[16,16,128]{2,1,0:T(8,128)S(1)} %merge.3), channel_id=1, replica_groups=mesh['z'=16,'x'=4,'c'=2,'t'=4] {'z'}, dimensions={0} | all-to-all | bytes 262144 | tf_op jit(solution)/shard_map/all_to_all | solution.py:408
  64.0 0.0 copy-done.6
  64.0 0.0 copy-done.2
  64.0 1.5 rows.2
  65.5 7.9 %all_to_all.57.partials = f32[4,4,128]{2,1,0:T(4,128)S(1)} all-to-all(f32[4,4,128]{2,1,0:T(4,128)S(1)} %get-tuple-element.25), channel_id=1, replica_groups=mesh['z'=16,'x'=4,'c'=2,'t'=4] {'t'}, dimensions={0} | all-to-all | bytes 16384 | tf_op jit(solution)/shard_map/all_to_all | solution.py:398
  73.4 0.0 copy-done.11
  73.4 1.4 cols.4
  74.9 8.0 %all_to_all.58.partials = f32[8,16,128]{2,1,0:T(8,128)S(1)} all-to-all(f32[8,16,128]{2,1,0:T(8,128)S(1)} %get-tuple-element.27), channel_id=1, replica_groups=mesh['z'=16,'x'=4,'c'=2,'t'=4] {'x','c'}, dimensions={0} | all-to-all | bytes 131072 | tf_op jit(solution)/shard_map/all_to_all | solution.py:406
  82.9 18.2 %all_to_all.59.partials = f32[16,16,128]{2,1,0:T(8,128)S(1)} all-to-all(f32[16,16,128]{2,1,0:T(8,128)S(1)} %merge.4), channel_id=1, replica_groups=mesh['z'=16,'x'=4,'c'=2,'t'=4] {'z'}, dimensions={0} | all-to-all | bytes 262144 | tf_op jit(solution)/shard_map/all_to_all | solution.py:408
  101.2 0.0 copy-start.4
  101.2 0.0 copy-start.9
  101.2 1.5 rows.3
  102.7 8.0 %all_to_all.60.partials = f32[4,4,128]{2,1,0:T(4,128)S(1)} all-to-all(f32[4,4,128]{2,1,0:T(4,128)S(1)} %get-tuple-element.29), channel_id=1, replica_groups=mesh['z'=16,'x'=4,'c'=2,'t'=4] {'t'}, dimensions={0} | all-to-all | bytes 16384 | tf_op jit(solution)/shard_map/all_to_all | solution.py:398
  110.7 1.4 cols.5
  112.1 7.7 %all_to_all.61.partials = f32[8,16,128]{2,1,0:T(8,128)S(1)} all-to-all(f32[8,16,128]{2,1,0:T(8,128)S(1)} %get-tuple-element.31), channel_id=1, replica_groups=mesh['z'=16,'x'=4,'c'=2,'t'=4] {'x','c'}, dimensions={0} | all-to-all | bytes 131072 | tf_op jit(solution)/shard_map/all_to_all | solution.py:406
  119.9 18.4 %all_to_all.62.partials = f32[16,16,128]{2,1,0:T(8,128)S(1)} all-to-all(f32[16,16,128]{2,1,0:T(8,128)S(1)} %merge.5), channel_id=1, replica_groups=mesh['z'=16,'x'=4,'c'=2,'t'=4] {'z'}, dimensions={0} | all-to-all | bytes 262144 | tf_op jit(solution)/shard_map/all_to_all | solution.py:408
  138.3 0.0 copy-done.4
  138.3 0.0 copy-done.9
  138.3 3.0 %mapping.1 = (f32[4,136,256]{2,1,0:T(8,128)S(1)}, f32[4,128]{1,0:T(4,128)}, f32[16,128]{1,0:T(8,128)}) custom-call(s32[32]{0:T(128)S(1)} %bitcast.23, s32[1]{0:T(128)} %bitcast.13.counts_hbm, f32[4,16,128,128]{3,2,1,0:T(8,128)S(1)} %copy-done.2, f32[16,16,128]{2,1,0:T(8,128)S(1)} %all_to_all.62.partials, f32[16,128]{1,0:T(8,128)S(1)} %bitcast.16, ...), custom_call_target="tpu_custom_call" | custom-call | flops 1000000 | bytes 2000000 | tf_op jit(solution)/shard_map/mapping/pallas_call | solution.py:417
  141.3 10.9 %all_to_all.63.packets = f32[4,136,256]{2,1,0:T(8,128)S(1)} all-to-all(f32[4,136,256]{2,1,0:T(8,128)S(1)} %get-tuple-element.36), channel_id=1, replica_groups=mesh['z'=16,'x'=4,'c'=2,'t'=4] {'t'}, dimensions={0} | all-to-all | bytes 1114112 | tf_op jit(solution)/shard_map/all_to_all | solution.py:425
  152.2 0.2 mix.1
  152.4 10.5 %all_to_all.64 = f32[4,128,256]{2,1,0:T(8,128)S(1)} all-to-all(f32[4,128,256]{2,1,0:T(8,128)S(1)} %mix.1), channel_id=1, replica_groups=mesh['z'=16,'x'=4,'c'=2,'t'=4] {'t'}, dimensions={0} | all-to-all | bytes 1048576 | tf_op jit(solution)/shard_map/all_to_all | solution.py:427
  162.9 0.8 copy.11
  (4 shorter events, 0.1 us)
Async XLA Ops:
  1.3 1.2 copy-start.3
  2.5 0.9 copy-start.5
  3.5 0.7 copy-start.7
  4.1 59.9 %copy-start.6 = (f32[2048]{0:T(1024)S(1)}, f32[2048]{0:T(1024)}, u32[]{:S(2)}) copy-start(f32[2048]{0:T(1024)} %param.9) | copy-start | bytes 24580
  9.4 1.9 %copy-start = (f32[4,16,128,128]{3,2,1,0:T(8,128)}, f32[4,16,128,128]{3,2,1,0:T(8,128)S(1)}, u32[]{:S(2)}) copy-start(f32[4,16,128,128]{3,2,1,0:T(8,128)S(1)} %get-tuple-element.20.gram) | copy-start | bytes 12582916
  11.3 9.6 %all-to-all-start = ((f32[4,4,128]{2,1,0:T(4,128)}), f32[4,4,128]{2,1,0:T(4,128)S(1)}, u32[]{:S(2)}, u32[]{:S(2)}) async-start(f32[4,4,128]{2,1,0:T(4,128)} %get-tuple-element.21), calls=%async_computation | async-start | bytes 16384 | tf_op jit(solution)/shard_map/all_to_all | solution.py:398
  21.0 2.2 %copy-start.1 = (f32[4,16,128,128]{3,2,1,0:T(8,128)S(1)}, f32[4,16,128,128]{3,2,1,0:T(8,128)}, u32[]{:S(2)}) copy-start(f32[4,16,128,128]{3,2,1,0:T(8,128)} %copy-done) | copy-start | bytes 12582916
  23.2 0.7 copy-start.8
  23.8 0.7 copy-start.10
  24.5 39.5 %copy-start.2 = (f32[4,16,128,128]{3,2,1,0:T(8,128)S(1)}, f32[4,16,128,128]{3,2,1,0:T(8,128)}, u32[]{:S(2)}) copy-start(f32[4,16,128,128]{3,2,1,0:T(8,128)} %copy-done) | copy-start | bytes 12582916
  24.5 48.9 %copy-start.11 = (f32[512]{0:T(512)S(1)}, f32[512]{0:T(512)}, u32[]{:S(2)}) copy-start(f32[512]{0:T(512)} %param.8) | copy-start | bytes 6148
  101.2 37.1 %copy-start.4 = (bf16[2048,256]{1,0:T(8,128)(2,1)S(1)}, bf16[2048,256]{1,0:T(8,128)(2,1)}, u32[]{:S(2)}) copy-start(bf16[2048,256]{1,0:T(8,128)(2,1)} %y.3) | copy-start | bytes 3145732
  101.2 37.1 %copy-start.9 = (s32[1,1,32]{2,1,0:T(1,128)S(1)}, s32[1,1,32]{2,1,0:T(1,128)}, u32[]{:S(2)}) copy-start(s32[1,1,32]{2,1,0:T(1,128)} %param.10) | copy-start | bytes 388

commit v3 on v2

--- a/solution.py
+++ b/solution.py
@@ -21,6 +21,8 @@
 VMEM = pl.BlockSpec(memory_space=pltpu.VMEM)
 ANY = pl.BlockSpec(memory_space=pl.ANY)
 OFFSET = 70.0
+ROW_STEP = 4
+COL_STEP = 4
 LEAST = 1e-28
 MOST = 1e37
 FIRST_LIMIT = 52
@@ -59,6 +61,21 @@
     return counts[0]
 
 
+def each(live, step, body):
+    whole = live >> (step.bit_length() - 1)
+
+    def several(i, unused):
+        body([i * step + j for j in range(step)])
+        return unused
+
+    def single(k, unused):
+        body([k])
+        return unused
+
+    lax.fori_loop(0, whole, several, 0)
+    lax.fori_loop(whole * step, live, single, 0)
+
+
 def entry(pairs, k):
     value = pairs[k]
     return value >> 4, value & 15
@@ -126,14 +143,14 @@
 def row_pass(pairs, live, gram, spread, before, row_spread, sums, found, peaks, also):
     sums[...] = jnp.zeros(sums.shape, jnp.float32)
 
-    def only(k, unused):
-        p, q = entry(pairs, k)
-        weight = jnp.exp(row_scores(gram, spread, p, q) + row_spread[p])
-        sums[p] += weight
-        also(p, q, weight)
-        return unused
-
-    lax.fori_loop(0, live, only, 0)
+    def only(slots):
+        places = [entry(pairs, k) for k in slots]
+        weights = [jnp.exp(row_scores(gram, spread, p, q) + row_spread[p]) for p, q in places]
+        for (p, q), weight in zip(places, weights):
+            sums[p] += weight
+            also(p, q, weight)
+
+    each(live, ROW_STEP, only)
     totals = row_totals(sums)
     found[...] = jnp.log(totals) - (before + OFFSET)
 
@@ -161,7 +178,7 @@
     gram,
     partial,
     x_norm,
-    y_norm,
+    y_start,
     pairs,
     counts,
     done,
@@ -175,8 +192,8 @@
     for p in range(SB):
         x_norm[pl.ds(p, 1)] = folded(x[pl.ds(p * BLOCK, BLOCK), :])
 
-    def chunk(c, unused):
-        cells = y[pl.ds(pl.multiple_of(c * 2 * BLOCK, 2 * BLOCK), 2 * BLOCK), :]
+    def chunk(c):
+        cells = y[pl.ds(c * 2 * BLOCK, 2 * BLOCK), :]
         dims = (((1,), (1,)), ((), ()))
         crossed = lax.dot_general(x[...], cells, dims, preferred_element_type=jnp.float32)
         crossed = crossed * (2.0 / (E * EPS))
@@ -187,10 +204,10 @@
                 gram[p, 2 * c + half] = crossed[
                     p * BLOCK : (p + 1) * BLOCK, half * BLOCK : (half + 1) * BLOCK
                 ]
-        return unused
-
-    lax.fori_loop(0, TB // 2, chunk, 0)
-    y_norm[...] = -spread[...][:, 0]
+
+    for c in range(TB // 2):
+        chunk(c)
+    y_start[...] = spread[...][:, 0]
     before = -x_norm[...]
     spread_rows(before + OFFSET, row_spread)
     live = fetched(lists, counts)
@@ -227,12 +244,13 @@
     def scores(p, q):
         return (spread[p] + gram[p, q]).reshape(BLOCK // 8, 8, BLOCK)
 
-    def only(k, unused):
-        p, q = entry(pairs, k)
-        sums[q] += jnp.sum(jnp.exp(scores(p, q) + col_spread[q][None]), axis=0)
-        return unused
-
-    lax.fori_loop(0, live, only, 0)
+    def only(slots):
+        places = [entry(pairs, k) for k in slots]
+        parts = [jnp.sum(jnp.exp(scores(p, q) + col_spread[q][None]), axis=0) for p, q in places]
+        for (p, q), part in zip(places, parts):
+            sums[q] += part
+
+    each(live, COL_STEP, only)
     totals = jnp.sum(sums[...], axis=1)
     found[...] = jnp.log(totals) - (before[...] + OFFSET)
 
@@ -304,7 +322,7 @@
     mass,
     before,
     x_norm,
-    y_norm,
+    y_start,
     y,
     packet,
     row_pot,
@@ -325,7 +343,7 @@
     lists = fetch(pairs_hbm, counts_hbm, pairs, counts, done)
     potential = jnp.log(mass[...]) - log_sum(partials[...])
     rows_out[...] = EPS * (before[...] + x_norm[...])
-    cols_out[...] = EPS * (potential + y_norm[...])
+    cols_out[...] = EPS * (potential - y_start[...])
     copies = [
         pltpu.make_async_copy(rows_out, row_pot, done.at[2]),
         pltpu.make_async_copy(cols_out, col_pot, done.at[3]),
@@ -386,14 +404,14 @@
     def sems(count):
         return pltpu.SemaphoreType.DMA((count,))
 
-    gram, row_part, x_norm, y_norm = call(
+    gram, row_part, x_norm, y_start = call(
         gram_kernel,
         (f32(SB, TB, BLOCK, BLOCK), f32(SB, SB, BLOCK), f32(SB, BLOCK), f32(TB, BLOCK)),
         lists + [sems(2), flat, tall, tall, tall, rows],
         "gram",
         [ANY] * 2 + [VMEM] * 2,
     )(pairs, counts, source_cells, target_cells)
-    col_pot = -y_norm
+    col_pot = y_start
     for iteration in range(ITERS):
         row_parts = lax.all_to_all(row_part, "t", 0, 0)
         col_part, row_pot = call(
@@ -421,7 +439,7 @@
         "mapping",
         [ANY] * 2 + [VMEM] * 7,
         out_specs=(VMEM, ANY, ANY),
-    )(pairs, counts, gram, col_parts, target_mass, row_pot, x_norm, y_norm, target_cells)
+    )(pairs, counts, gram, col_parts, target_mass, row_pot, x_norm, y_start, target_cells)
     packets = lax.all_to_all(packet, "t", 0, 0)
     quarters = call(mix_kernel, f32(SB, BLOCK, E), [], "mix", [VMEM])(packets)
     mapped = lax.all_to_all(quarters, "t", 0, 0)

time: 164 us -> 159 us (0.970)
  the two profiles are of different devices: /device:TPU:2 before, /device:TPU:32 now
where the time goes in v3:
time: 159 us; the launch traced here: 158 us
  blocking collectives  140 us (88%)
  Pallas kernels  12.4 us (8%)
  local copies, waits for them, and re-layouts  4.3 us (3%)
    all_to_all x3, blocking collectives, shards(): col_parts = lax.all_to_all(col_parts, 'z', 0, 0)  64.9 us
    all_to_all x3, blocking collectives, shards(): row_parts = lax.all_to_all(row_part, 't', 0, 0)  27 us
    all_to_all x3, blocking collectives, shards(): col_parts = lax.all_to_all(col_part, ('x', 'c'), 0, 0)  25.7 us
    all_to_all x1, blocking collectives, shards(): packets = lax.all_to_all(packet, 't', 0, 0)  12 us
    all_to_all x1, blocking collectives, shards(): mapped = lax.all_to_all(quarters, 't', 0, 0)  10.5 us
    unnamed x13, local copies, waits for them, and re-layouts  4.3 us
    pallas_call x3, Pallas kernels, shards(): call(col_kernel, (f32(XC, TB, BLOCK), f32(SB, BLOCK)), lists + [sems(2),...  4.03 us

profile of v3, /device:TPU:32, one launch (start us, length us, event | category | flops | bytes accessed | tf_op | source)
XLA Modules:
  0.0 158.0 jit_solution(14515741730622921625)
XLA Ops:
  0.6 0.0 copy-start.4
  1.3 0.0 copy-start
  1.3 1.2 copy-done
  2.5 0.0 copy-start.1
  2.5 0.9 copy-done.1
  3.5 0.0 copy-start.3
  3.5 0.7 copy-done.3
  4.1 0.0 copy-start.2
  4.1 2.9 %gram.1 = (f32[4,16,128,128]{3,2,1,0:T(8,128)S(1)}, f32[4,4,128]{2,1,0:T(4,128)S(1)}, f32[4,128]{1,0:T(4,128)S(1)}, f32[16,128]{1,0:T(8,128)S(1)}) custom-call(s32[32]{0:T(128)S(1)} %bitcast.17, s32[1]{0:T(128)} %bitcast.7.counts_hbm, bf16[512,256]{1,0:T(8,128)(2,1)S(1)} %copy-done.1, bf16[2048,256]{1,0:T(8,128)(2,1)S(1)} %copy-done), custom_call_target="tpu_custom_call" | custom-call | flops 1000000 | bytes 2000000 | tf_op jit(solution)/shard_map/gram/pallas_call | solution.py:407
  7.1 10.1 %all_to_all.55.partials = f32[4,4,128]{2,1,0:T(4,128)S(1)} all-to-all(f32[4,4,128]{2,1,0:T(4,128)S(1)} %get-tuple-element.21), channel_id=1, replica_groups=mesh['z'=16,'x'=4,'c'=2,'t'=4] {'t'}, dimensions={0} | all-to-all | bytes 16384 | tf_op jit(solution)/shard_map/all_to_all | solution.py:416
  17.2 0.0 copy-start.5
  17.2 0.7 copy-done.5
  17.9 2.0 %cols.3 = (f32[8,16,128]{2,1,0:T(8,128)S(1)}, f32[4,128]{1,0:T(4,128)S(1)}) custom-call(s32[32]{0:T(128)S(1)} %bitcast.18, s32[1]{0:T(128)} %bitcast.8.counts_hbm, f32[4,16,128,128]{3,2,1,0:T(8,128)S(1)} %get-tuple-element.20.gram, f32[4,4,128]{2,1,0:T(4,128)S(1)} %all_to_all.55.partials, f32[4,128]{1,0:T(4,128)S(1)} %bitcast.24, ...), custom_call_target="tpu_custom_call" | custom-call | flops 1000000 | bytes 2000000 | tf_op jit(solution)/shard_map/cols/pallas_call | solution.py:417
  19.8 9.7 %all_to_all.56.partials = f32[8,16,128]{2,1,0:T(8,128)S(1)} all-to-all(f32[8,16,128]{2,1,0:T(8,128)S(1)} %get-tuple-element.23), channel_id=1, replica_groups=mesh['z'=16,'x'=4,'c'=2,'t'=4] {'x','c'}, dimensions={0} | all-to-all | bytes 131072 | tf_op jit(solution)/shard_map/all_to_all | solution.py:424
  29.5 28.5 %all_to_all.57.partials = f32[16,16,128]{2,1,0:T(8,128)S(1)} all-to-all(f32[16,16,128]{2,1,0:T(8,128)S(1)} %merge.3), channel_id=1, replica_groups=mesh['z'=16,'x'=4,'c'=2,'t'=4] {'z'}, dimensions={0} | all-to-all | bytes 262144 | tf_op jit(solution)/shard_map/all_to_all | solution.py:426
  58.0 0.0 copy-done.4
  58.0 0.0 copy-done.2
  58.0 1.2 rows.2
  59.3 8.0 %all_to_all.58.partials = f32[4,4,128]{2,1,0:T(4,128)S(1)} all-to-all(f32[4,4,128]{2,1,0:T(4,128)S(1)} %get-tuple-element.25), channel_id=1, replica_groups=mesh['z'=16,'x'=4,'c'=2,'t'=4] {'t'}, dimensions={0} | all-to-all | bytes 16384 | tf_op jit(solution)/shard_map/all_to_all | solution.py:416
  67.3 1.0 cols.4
  68.3 8.0 %all_to_all.59.partials = f32[8,16,128]{2,1,0:T(8,128)S(1)} all-to-all(f32[8,16,128]{2,1,0:T(8,128)S(1)} %get-tuple-element.27), channel_id=1, replica_groups=mesh['z'=16,'x'=4,'c'=2,'t'=4] {'x','c'}, dimensions={0} | all-to-all | bytes 131072 | tf_op jit(solution)/shard_map/all_to_all | solution.py:424
  76.4 18.2 %all_to_all.60.partials = f32[16,16,128]{2,1,0:T(8,128)S(1)} all-to-all(f32[16,16,128]{2,1,0:T(8,128)S(1)} %merge.4), channel_id=1, replica_groups=mesh['z'=16,'x'=4,'c'=2,'t'=4] {'z'}, dimensions={0} | all-to-all | bytes 262144 | tf_op jit(solution)/shard_map/all_to_all | solution.py:426
  94.5 1.2 rows.3
  95.8 8.9 %all_to_all.61.partials = f32[4,4,128]{2,1,0:T(4,128)S(1)} all-to-all(f32[4,4,128]{2,1,0:T(4,128)S(1)} %get-tuple-element.29), channel_id=1, replica_groups=mesh['z'=16,'x'=4,'c'=2,'t'=4] {'t'}, dimensions={0} | all-to-all | bytes 16384 | tf_op jit(solution)/shard_map/all_to_all | solution.py:416
  104.6 1.0 cols.5
  105.7 8.0 %all_to_all.62.partials = f32[8,16,128]{2,1,0:T(8,128)S(1)} all-to-all(f32[8,16,128]{2,1,0:T(8,128)S(1)} %get-tuple-element.31), channel_id=1, replica_groups=mesh['z'=16,'x'=4,'c'=2,'t'=4] {'x','c'}, dimensions={0} | all-to-all | bytes 131072 | tf_op jit(solution)/shard_map/all_to_all | solution.py:424
  113.7 18.2 %all_to_all.63.partials = f32[16,16,128]{2,1,0:T(8,128)S(1)} all-to-all(f32[16,16,128]{2,1,0:T(8,128)S(1)} %merge.5), channel_id=1, replica_groups=mesh['z'=16,'x'=4,'c'=2,'t'=4] {'z'}, dimensions={0} | all-to-all | bytes 262144 | tf_op jit(solution)/shard_map/all_to_all | solution.py:426
  131.9 2.7 %mapping.1 = (f32[4,136,256]{2,1,0:T(8,128)S(1)}, f32[4,128]{1,0:T(4,128)}, f32[16,128]{1,0:T(8,128)}) custom-call(s32[32]{0:T(128)S(1)} %bitcast.23, s32[1]{0:T(128)} %bitcast.13.counts_hbm, f32[4,16,128,128]{3,2,1,0:T(8,128)S(1)} %get-tuple-element.20.gram, f32[16,16,128]{2,1,0:T(8,128)S(1)} %all_to_all.63.partials, f32[16,128]{1,0:T(8,128)S(1)} %bitcast.16, ...), custom_call_target="tpu_custom_call" | custom-call | flops 1000000 | bytes 2000000 | tf_op jit(solution)/shard_map/mapping/pallas_call | solution.py:435
  134.6 12.0 %all_to_all.64.packets = f32[4,136,256]{2,1,0:T(8,128)S(1)} all-to-all(f32[4,136,256]{2,1,0:T(8,128)S(1)} %get-tuple-element.36), channel_id=1, replica_groups=mesh['z'=16,'x'=4,'c'=2,'t'=4] {'t'}, dimensions={0} | all-to-all | bytes 1114112 | tf_op jit(solution)/shard_map/all_to_all | solution.py:443
  146.6 0.2 mix.1
  146.8 10.5 %all_to_all.65 = f32[4,128,256]{2,1,0:T(8,128)S(1)} all-to-all(f32[4,128,256]{2,1,0:T(8,128)S(1)} %mix.1), channel_id=1, replica_groups=mesh['z'=16,'x'=4,'c'=2,'t'=4] {'t'}, dimensions={0} | all-to-all | bytes 1048576 | tf_op jit(solution)/shard_map/all_to_all | solution.py:445
  157.3 0.8 copy.11
  (3 shorter events, 0.1 us)
Async XLA Ops:
  0.6 57.4 %copy-start.4 = (s32[1,1,32]{2,1,0:T(1,128)S(1)}, s32[1,1,32]{2,1,0:T(1,128)}, u32[]{:S(2)}) copy-start(s32[1,1,32]{2,1,0:T(1,128)} %param.10) | copy-start | bytes 388
  1.3 1.2 copy-start
  2.5 0.9 copy-start.1
  3.5 0.7 copy-start.3
  4.1 53.9 %copy-start.2 = (f32[2048]{0:T(1024)S(1)}, f32[2048]{0:T(1024)}, u32[]{:S(2)}) copy-start(f32[2048]{0:T(1024)} %param.9) | copy-start | bytes 24580
  17.2 0.7 copy-start.5

commit v4 on v3

--- a/solution.py
+++ b/solution.py
@@ -21,6 +21,7 @@
 VMEM = pl.BlockSpec(memory_space=pltpu.VMEM)
 ANY = pl.BlockSpec(memory_space=pl.ANY)
 OFFSET = 70.0
+FIRST = 5000000000
 ROW_STEP = 4
 COL_STEP = 4
 LEAST = 1e-28
@@ -28,7 +29,7 @@
 FIRST_LIMIT = 52
 
 
-def call(kernel, out_shape, scratch, name, specs, out_specs=None):
+def call(kernel, out_shape, scratch, name, specs, out_specs=None, flops=1000000):
     return pl.pallas_call(
         kernel,
         out_shape=out_shape,
@@ -36,7 +37,7 @@
         out_specs=out_specs or jax.tree.map(lambda unused: VMEM, out_shape),
         scratch_shapes=scratch,
         compiler_params=pltpu.CompilerParams(vmem_limit_bytes=16 * 1024 * 1024),
-        cost_estimate=pl.CostEstimate(flops=1000000, bytes_accessed=2000000, transcendentals=500000),
+        cost_estimate=pl.CostEstimate(flops=flops, bytes_accessed=2000000, transcendentals=500000),
         name=name,
     )
 
@@ -170,15 +171,22 @@
     return None
 
 
+def zero_kernel(zeros):
+    zeros[...] = jnp.zeros(zeros.shape, jnp.float32)
+
+
 def gram_kernel(
     pairs_hbm,
     counts_hbm,
     x,
     y,
+    mass,
+    zeros,
     gram,
     partial,
     x_norm,
     y_start,
+    log_mass,
     pairs,
     counts,
     done,
@@ -188,6 +196,7 @@
     sums,
     found,
 ):
+    log_mass[...] = jnp.log(mass[...])
     lists = fetch(pairs_hbm, counts_hbm, pairs, counts, done)
     for p in range(SB):
         x_norm[pl.ds(p, 1)] = folded(x[pl.ds(p * BLOCK, BLOCK), :])
@@ -208,7 +217,7 @@
     for c in range(TB // 2):
         chunk(c)
     y_start[...] = spread[...][:, 0]
-    before = -x_norm[...]
+    before = zeros[...] - x_norm[...]
     spread_rows(before + OFFSET, row_spread)
     live = fetched(lists, counts)
     row_pass(pairs, live, gram, spread, before, row_spread, sums, found, peaks, nothing)
@@ -221,7 +230,7 @@
     counts_hbm,
     gram,
     partials,
-    mass,
+    mass_log,
     before,
     partial,
     potential,
@@ -235,7 +244,7 @@
     found,
 ):
     lists = fetch(pairs_hbm, counts_hbm, pairs, counts, done)
-    potential[...] = jnp.log(mass[...]) - log_sum(partials[...])
+    potential[...] = mass_log[...] - log_sum(partials[...])
     spread_rows(potential[...], spread)
     spread_cols(before[...] + OFFSET, col_spread)
     sums[...] = jnp.zeros(sums.shape, jnp.float32)
@@ -275,7 +284,7 @@
         lax.fori_loop(0, live, second, 0)
         found[...] = peaks[...][:, 0] + jnp.log(jnp.sum(sums[...], axis=1))
 
-    for d in range(XC):
+    for d in range(Z):
         partial[d] = found[...]
 
 
@@ -404,26 +413,33 @@
     def sems(count):
         return pltpu.SemaphoreType.DMA((count,))
 
-    gram, row_part, x_norm, y_start = call(
+    zeros = call(zero_kernel, f32(SB, BLOCK), [], "zeros", [], flops=FIRST)()
+    gram, row_part, x_norm, y_start, source_log = call(
         gram_kernel,
-        (f32(SB, TB, BLOCK, BLOCK), f32(SB, SB, BLOCK), f32(SB, BLOCK), f32(TB, BLOCK)),
+        (
+            f32(SB, TB, BLOCK, BLOCK),
+            f32(SB, SB, BLOCK),
+            f32(SB, BLOCK),
+            f32(TB, BLOCK),
+            f32(SB, BLOCK),
+        ),
         lists + [sems(2), flat, tall, tall, tall, rows],
         "gram",
-        [ANY] * 2 + [VMEM] * 2,
-    )(pairs, counts, source_cells, target_cells)
+        [ANY] * 2 + [VMEM] * 4,
+    )(pairs, counts, source_cells, target_cells, source_mass, zeros)
     col_pot = y_start
     for iteration in range(ITERS):
         row_parts = lax.all_to_all(row_part, "t", 0, 0)
         col_part, row_pot = call(
             col_kernel,
-            (f32(XC, TB, BLOCK), f32(SB, BLOCK)),
+            (f32(Z, TB, BLOCK), f32(SB, BLOCK)),
             lists + [sems(2), tall, flat, flat, flat, cols],
             "cols",
             [ANY] * 2 + [VMEM] * 4,
-        )(pairs, counts, gram, row_parts, source_mass, col_pot)
-        col_parts = lax.all_to_all(col_part, ("x", "c"), 0, 0)
-        col_parts = call(merge_kernel, f32(Z, TB, BLOCK), [], "merge", [VMEM])(col_parts)
-        col_parts = lax.all_to_all(col_parts, "z", 0, 0)
+        )(pairs, counts, gram, row_parts, source_log, col_pot)
+        col_parts = lax.all_to_all(col_part, "z", 0, 0)
+        col_parts = call(merge_kernel, f32(XC, TB, BLOCK), [], "merge", [VMEM])(col_parts)
+        col_parts = lax.all_to_all(col_parts, ("x", "c"), 0, 0)
         if iteration < ITERS - 1:
             row_part, col_pot = call(
                 row_kernel,

time: 159 us -> 152 us (0.956)
  the two profiles are of different devices: /device:TPU:32 before, /device:TPU:2 now
where the time goes in v4:
time: 152 us; the launch traced here: 151 us
  blocking collectives  137 us (90%)
  Pallas kernels  11.2 us (7%)
    all_to_all x3, blocking collectives, shards(): col_parts = lax.all_to_all(col_part, 'z', 0, 0)  63.7 us
    all_to_all x3, blocking collectives, shards(): col_parts = lax.all_to_all(col_parts, ('x', 'c'), 0, 0)  25.1 us
    all_to_all x3, blocking collectives, shards(): row_parts = lax.all_to_all(row_part, 't', 0, 0)  24.9 us
    all_to_all x1, blocking collectives, shards(): packets = lax.all_to_all(packet, 't', 0, 0)  12.5 us
    all_to_all x1, blocking collectives, shards(): mapped = lax.all_to_all(quarters, 't', 0, 0)  11.3 us

profile of v4, /device:TPU:2, one launch (start us, length us, event | category | flops | bytes accessed | tf_op | source)
XLA Modules:
  0.0 151.4 jit_solution(16991808371476071847)
XLA Ops:
  0.6 0.0 copy-start
  0.6 0.0 copy-start.3
  0.7 0.0 copy-start.4
  0.7 0.0 copy-start.1
  0.7 0.0 copy-start.2
  1.4 0.4 copy-done
  1.9 0.0 copy-done.3
  1.9 0.0 copy-done.4
  1.9 0.1 copy-done.1
  1.9 2.9 %gram.1 = (f32[4,16,128,128]{3,2,1,0:T(8,128)S(1)}, f32[4,4,128]{2,1,0:T(4,128)S(1)}, f32[4,128]{1,0:T(4,128)S(1)}, f32[16,128]{1,0:T(8,128)S(1)}, f32[4,128]{1,0:T(4,128)S(1)}) custom-call(s32[32]{0:T(128)S(1)} %bitcast.17, s32[1]{0:T(128)} %bitcast.7.counts_hbm, bf16[512,256]{1,0:T(8,128)(2,1)S(1)} %copy-done.1, bf16[2048,256]{1,0:T(8,128)(2,1)S(1)} %copy-done, ...), custom_call_target="tpu_custom_call" | custom-call | flops 1000000 | bytes 2000000 | tf_op jit(solution)/shard_map/gram/pallas_call | solution.py:417
  4.8 9.5 %all_to_all.55.partials = f32[4,4,128]{2,1,0:T(4,128)S(1)} all-to-all(f32[4,4,128]{2,1,0:T(4,128)S(1)} %get-tuple-element.22), channel_id=1, replica_groups=mesh['z'=16,'x'=4,'c'=2,'t'=4] {'t'}, dimensions={0} | all-to-all | bytes 16384 | tf_op jit(solution)/shard_map/all_to_all | solution.py:432
  14.4 1.0 cols.3
  15.4 29.2 %all_to_all.56.partials = f32[16,16,128]{2,1,0:T(8,128)S(1)} all-to-all(f32[16,16,128]{2,1,0:T(8,128)S(1)} %get-tuple-element.25), channel_id=1, replica_groups=mesh['z'=16,'x'=4,'c'=2,'t'=4] {'z'}, dimensions={0} | all-to-all | bytes 262144 | tf_op jit(solution)/shard_map/all_to_all | solution.py:440
  44.6 8.7 %all_to_all.57.partials = f32[8,16,128]{2,1,0:T(8,128)S(1)} all-to-all(f32[8,16,128]{2,1,0:T(8,128)S(1)} %merge.3), channel_id=1, replica_groups=mesh['z'=16,'x'=4,'c'=2,'t'=4] {'x','c'}, dimensions={0} | all-to-all | bytes 131072 | tf_op jit(solution)/shard_map/all_to_all | solution.py:442
  53.3 0.0 copy-done.2
  53.3 1.1 rows.2
  54.4 7.7 %all_to_all.58.partials = f32[4,4,128]{2,1,0:T(4,128)S(1)} all-to-all(f32[4,4,128]{2,1,0:T(4,128)S(1)} %get-tuple-element.27), channel_id=1, replica_groups=mesh['z'=16,'x'=4,'c'=2,'t'=4] {'t'}, dimensions={0} | all-to-all | bytes 16384 | tf_op jit(solution)/shard_map/all_to_all | solution.py:432
  62.1 1.0 cols.4
  63.1 17.3 %all_to_all.59.partials = f32[16,16,128]{2,1,0:T(8,128)S(1)} all-to-all(f32[16,16,128]{2,1,0:T(8,128)S(1)} %get-tuple-element.29), channel_id=1, replica_groups=mesh['z'=16,'x'=4,'c'=2,'t'=4] {'z'}, dimensions={0} | all-to-all | bytes 262144 | tf_op jit(solution)/shard_map/all_to_all | solution.py:440
  80.4 8.2 %all_to_all.60.partials = f32[8,16,128]{2,1,0:T(8,128)S(1)} all-to-all(f32[8,16,128]{2,1,0:T(8,128)S(1)} %merge.4), channel_id=1, replica_groups=mesh['z'=16,'x'=4,'c'=2,'t'=4] {'x','c'}, dimensions={0} | all-to-all | bytes 131072 | tf_op jit(solution)/shard_map/all_to_all | solution.py:442
  88.7 1.1 rows.3
  89.8 7.7 %all_to_all.61.partials = f32[4,4,128]{2,1,0:T(4,128)S(1)} all-to-all(f32[4,4,128]{2,1,0:T(4,128)S(1)} %get-tuple-element.31), channel_id=1, replica_groups=mesh['z'=16,'x'=4,'c'=2,'t'=4] {'t'}, dimensions={0} | all-to-all | bytes 16384 | tf_op jit(solution)/shard_map/all_to_all | solution.py:432
  97.5 1.0 cols.5
  98.5 17.2 %all_to_all.62.partials = f32[16,16,128]{2,1,0:T(8,128)S(1)} all-to-all(f32[16,16,128]{2,1,0:T(8,128)S(1)} %get-tuple-element.33), channel_id=1, replica_groups=mesh['z'=16,'x'=4,'c'=2,'t'=4] {'z'}, dimensions={0} | all-to-all | bytes 262144 | tf_op jit(solution)/shard_map/all_to_all | solution.py:440
  115.8 8.2 %all_to_all.63.partials = f32[8,16,128]{2,1,0:T(8,128)S(1)} all-to-all(f32[8,16,128]{2,1,0:T(8,128)S(1)} %merge.5), channel_id=1, replica_groups=mesh['z'=16,'x'=4,'c'=2,'t'=4] {'x','c'}, dimensions={0} | all-to-all | bytes 131072 | tf_op jit(solution)/shard_map/all_to_all | solution.py:442
  124.0 2.7 %mapping.1 = (f32[4,136,256]{2,1,0:T(8,128)S(1)}, f32[4,128]{1,0:T(4,128)}, f32[16,128]{1,0:T(8,128)}) custom-call(s32[32]{0:T(128)S(1)} %bitcast.23, s32[1]{0:T(128)} %bitcast.13.counts_hbm, f32[4,16,128,128]{3,2,1,0:T(8,128)S(1)} %get-tuple-element.21.gram, f32[8,16,128]{2,1,0:T(8,128)S(1)} %all_to_all.63.partials, f32[16,128]{1,0:T(8,128)S(1)} %bitcast.16, ...), custom_call_target="tpu_custom_call" | custom-call | flops 1000000 | bytes 2000000 | tf_op jit(solution)/shard_map/mapping/pallas_call | solution.py:451
  126.7 12.5 %all_to_all.64.packets = f32[4,136,256]{2,1,0:T(8,128)S(1)} all-to-all(f32[4,136,256]{2,1,0:T(8,128)S(1)} %get-tuple-element.38), channel_id=1, replica_groups=mesh['z'=16,'x'=4,'c'=2,'t'=4] {'t'}, dimensions={0} | all-to-all | bytes 1114112 | tf_op jit(solution)/shard_map/all_to_all | solution.py:459
  139.1 0.2 mix.1
  139.3 11.3 %all_to_all.65 = f32[4,128,256]{2,1,0:T(8,128)S(1)} all-to-all(f32[4,128,256]{2,1,0:T(8,128)S(1)} %mix.1), channel_id=1, replica_groups=mesh['z'=16,'x'=4,'c'=2,'t'=4] {'t'}, dimensions={0} | all-to-all | bytes 1048576 | tf_op jit(solution)/shard_map/all_to_all | solution.py:461
  150.6 0.8 copy.11
  (4 shorter events, 0.1 us)
Async XLA Ops:
  0.6 1.2 copy-start
  0.6 1.2 copy-start.3
  0.7 1.2 copy-start.4
  0.7 1.3 copy-start.1
  0.7 52.6 %copy-start.2 = (f32[2048]{0:T(1024)S(1)}, f32[2048]{0:T(1024)}, u32[]{:S(2)}) copy-start(f32[2048]{0:T(1024)} %param.9) | copy-start | bytes 24580

commit v5 on v4

--- a/solution.py
+++ b/solution.py
@@ -24,8 +24,8 @@
 FIRST = 5000000000
 ROW_STEP = 4
 COL_STEP = 4
-LEAST = 1e-28
-MOST = 1e37
+MIDDLE = 10.0
+REACH = 74.0
 FIRST_LIMIT = 52
 
 
@@ -46,20 +46,10 @@
     return jax.ShapeDtypeStruct(shape, jnp.float32)
 
 
-def fetch(pairs_hbm, counts_hbm, pairs, counts, done):
-    copies = [
-        pltpu.make_async_copy(pairs_hbm, pairs, done.at[0]),
-        pltpu.make_async_copy(counts_hbm, counts, done.at[1]),
-    ]
-    for copy in copies:
-        copy.start()
-    return copies
-
-
-def fetched(copies, counts):
-    for copy in copies:
-        copy.wait()
-    return counts[0]
+def fetch(listed, pairs):
+    for k in range(MAXB):
+        pairs[k] = listed[0, k]
+    return listed[1, 0]
 
 
 def each(live, step, body):
@@ -91,8 +81,8 @@
     return top + jnp.log(jnp.sum(jnp.exp(parts - top[None]), axis=0))
 
 
-def in_range(totals):
-    return jnp.logical_and(jnp.min(totals) >= LEAST, jnp.max(totals) <= MOST)
+def in_range(logs):
+    return jnp.max(jnp.abs(logs - MIDDLE)) <= REACH
 
 
 def spread_rows(potential, spread):
@@ -152,10 +142,10 @@
             also(p, q, weight)
 
     each(live, ROW_STEP, only)
-    totals = row_totals(sums)
-    found[...] = jnp.log(totals) - (before + OFFSET)
-
-    @pl.when(jnp.logical_not(in_range(totals)))
+    logs = jnp.log(row_totals(sums))
+    found[...] = logs - (before + OFFSET)
+
+    @pl.when(jnp.logical_not(in_range(logs)))
     def again():
         row_passes(pairs, live, gram, spread, peaks, sums, found, also)
 
@@ -176,8 +166,8 @@
 
 
 def gram_kernel(
-    pairs_hbm,
-    counts_hbm,
+    pairs_in,
+    counts,
     x,
     y,
     mass,
@@ -187,17 +177,18 @@
     x_norm,
     y_start,
     log_mass,
+    listed,
     pairs,
-    counts,
-    done,
     spread,
     row_spread,
     peaks,
     sums,
     found,
 ):
+    listed[...] = jnp.zeros(listed.shape, jnp.int32)
+    listed[pl.ds(0, 1), pl.ds(0, MAXB)] = pairs_in[...]
+    listed[pl.ds(1, 1), pl.ds(0, 1)] = counts[...]
     log_mass[...] = jnp.log(mass[...])
-    lists = fetch(pairs_hbm, counts_hbm, pairs, counts, done)
     for p in range(SB):
         x_norm[pl.ds(p, 1)] = folded(x[pl.ds(p * BLOCK, BLOCK), :])
 
@@ -219,15 +210,14 @@
     y_start[...] = spread[...][:, 0]
     before = zeros[...] - x_norm[...]
     spread_rows(before + OFFSET, row_spread)
-    live = fetched(lists, counts)
+    live = fetch(listed, pairs)
     row_pass(pairs, live, gram, spread, before, row_spread, sums, found, peaks, nothing)
     for d in range(SB):
         partial[d] = found[...]
 
 
 def col_kernel(
-    pairs_hbm,
-    counts_hbm,
+    listed,
     gram,
     partials,
     mass_log,
@@ -235,20 +225,17 @@
     partial,
     potential,
     pairs,
-    counts,
-    done,
     spread,
     col_spread,
     peaks,
     sums,
     found,
 ):
-    lists = fetch(pairs_hbm, counts_hbm, pairs, counts, done)
     potential[...] = mass_log[...] - log_sum(partials[...])
     spread_rows(potential[...], spread)
     spread_cols(before[...] + OFFSET, col_spread)
     sums[...] = jnp.zeros(sums.shape, jnp.float32)
-    live = fetched(lists, counts)
+    live = fetch(listed, pairs)
 
     def scores(p, q):
         return (spread[p] + gram[p, q]).reshape(BLOCK // 8, 8, BLOCK)
@@ -260,10 +247,10 @@
             sums[q] += part
 
     each(live, COL_STEP, only)
-    totals = jnp.sum(sums[...], axis=1)
-    found[...] = jnp.log(totals) - (before[...] + OFFSET)
-
-    @pl.when(jnp.logical_not(in_range(totals)))
+    logs = jnp.log(jnp.sum(sums[...], axis=1))
+    found[...] = logs - (before[...] + OFFSET)
+
+    @pl.when(jnp.logical_not(in_range(logs)))
     def again():
         peaks[...] = jnp.full(peaks.shape, -jnp.inf, jnp.float32)
         sums[...] = jnp.zeros(sums.shape, jnp.float32)
@@ -294,8 +281,7 @@
 
 
 def row_kernel(
-    pairs_hbm,
-    counts_hbm,
+    listed,
     gram,
     partials,
     mass,
@@ -303,19 +289,16 @@
     partial,
     potential,
     pairs,
-    counts,
-    done,
     spread,
     row_spread,
     peaks,
     sums,
     found,
 ):
-    lists = fetch(pairs_hbm, counts_hbm, pairs, counts, done)
     potential[...] = jnp.log(mass[...]) - log_sum(partials[...])
     spread_cols(potential[...], spread)
     spread_rows(before[...] + OFFSET, row_spread)
-    live = fetched(lists, counts)
+    live = fetch(listed, pairs)
     row_pass(
         pairs, live, gram, spread, before[...], row_spread, sums, found, peaks, nothing
     )
@@ -324,8 +307,7 @@
 
 
 def map_kernel(
-    pairs_hbm,
-    counts_hbm,
+    listed,
     gram,
     partials,
     mass,
@@ -337,7 +319,6 @@
     row_pot,
     col_pot,
     pairs,
-    counts,
     done,
     spread,
     row_spread,
@@ -349,13 +330,12 @@
     rows_out,
     cols_out,
 ):
-    lists = fetch(pairs_hbm, counts_hbm, pairs, counts, done)
     potential = jnp.log(mass[...]) - log_sum(partials[...])
     rows_out[...] = EPS * (before[...] + x_norm[...])
     cols_out[...] = EPS * (potential - y_start[...])
     copies = [
-        pltpu.make_async_copy(rows_out, row_pot, done.at[2]),
-        pltpu.make_async_copy(cols_out, col_pot, done.at[3]),
+        pltpu.make_async_copy(rows_out, row_pot, done.at[0]),
+        pltpu.make_async_copy(cols_out, col_pot, done.at[1]),
     ]
     for copy in copies:
         copy.start()
@@ -371,7 +351,7 @@
         high[rows, cols] = leading
         low[rows, cols] = (weight - leading.astype(jnp.float32)).astype(jnp.bfloat16)
 
-    live = fetched(lists, counts)
+    live = fetch(listed, pairs)
     row_pass(pairs, live, gram, spread, before[...], row_spread, sums, found, peaks, also)
     total = jnp.dot(high[...], y[...], preferred_element_type=jnp.float32) + jnp.dot(
         low[...], y[...], preferred_element_type=jnp.float32
@@ -399,8 +379,8 @@
 
 
 def shards(source_cells, target_cells, source_mass, target_mass, pairs, counts):
-    pairs = pairs.reshape(MAXB)
-    counts = counts.reshape(1)
+    pairs = pairs.reshape(1, MAXB)
+    counts = counts.reshape(1, 1)
     source_mass = source_mass.reshape(SB, BLOCK)
     target_mass = target_mass.reshape(TB, BLOCK)
     tall = pltpu.VMEM((SB, BLOCK, BLOCK), jnp.float32)
@@ -408,13 +388,13 @@
     rows = pltpu.VMEM((SB, BLOCK), jnp.float32)
     cols = pltpu.VMEM((TB, BLOCK), jnp.float32)
     dense = pltpu.VMEM((SB * BLOCK, TB * BLOCK), jnp.bfloat16)
-    lists = [pltpu.SMEM((MAXB,), jnp.int32), pltpu.SMEM((1,), jnp.int32)]
+    lists = [pltpu.SMEM((MAXB,), jnp.int32)]
 
     def sems(count):
         return pltpu.SemaphoreType.DMA((count,))
 
     zeros = call(zero_kernel, f32(SB, BLOCK), [], "zeros", [], flops=FIRST)()
-    gram, row_part, x_norm, y_start, source_log = call(
+    gram, row_part, x_norm, y_start, source_log, listed = call(
         gram_kernel,
         (
             f32(SB, TB, BLOCK, BLOCK),
@@ -422,10 +402,11 @@
             f32(SB, BLOCK),
             f32(TB, BLOCK),
             f32(SB, BLOCK),
+            jax.ShapeDtypeStruct((8, BLOCK), jnp.int32),
         ),
-        lists + [sems(2), flat, tall, tall, tall, rows],
+        lists + [flat, tall, tall, tall, rows],
         "gram",
-        [ANY] * 2 + [VMEM] * 4,
+        [VMEM] * 6,
     )(pairs, counts, source_cells, target_cells, source_mass, zeros)
     col_pot = y_start
     for iteration in range(ITERS):
@@ -433,10 +414,10 @@
         col_part, row_pot = call(
             col_kernel,
             (f32(Z, TB, BLOCK), f32(SB, BLOCK)),
-            lists + [sems(2), tall, flat, flat, flat, cols],
+            lists + [tall, flat, flat, flat, cols],
             "cols",
-            [ANY] * 2 + [VMEM] * 4,
-        )(pairs, counts, gram, row_parts, source_log, col_pot)
+            [VMEM] + [VMEM] * 4,
+        )(listed, gram, row_parts, source_log, col_pot)
         col_parts = lax.all_to_all(col_part, "z", 0, 0)
         col_parts = call(merge_kernel, f32(XC, TB, BLOCK), [], "merge", [VMEM])(col_parts)
         col_parts = lax.all_to_all(col_parts, ("x", "c"), 0, 0)
@@ -444,18 +425,18 @@
             row_part, col_pot = call(
                 row_kernel,
                 (f32(SB, SB, BLOCK), f32(TB, BLOCK)),
-                lists + [sems(2), flat, tall, tall, tall, rows],
+                lists + [flat, tall, tall, tall, rows],
                 "rows",
-                [ANY] * 2 + [VMEM] * 4,
-            )(pairs, counts, gram, col_parts, target_mass, row_pot)
+                [VMEM] + [VMEM] * 4,
+            )(listed, gram, col_parts, target_mass, row_pot)
     packet, row_pot, col_pot = call(
         map_kernel,
         (f32(SB, BLOCK + 8, E), f32(SB, BLOCK), f32(TB, BLOCK)),
-        lists + [sems(4), flat, tall, tall, tall, rows, dense, dense, rows, cols],
+        lists + [sems(2), flat, tall, tall, tall, rows, dense, dense, rows, cols],
         "mapping",
-        [ANY] * 2 + [VMEM] * 7,
+        [VMEM] + [VMEM] * 7,
         out_specs=(VMEM, ANY, ANY),
-    )(pairs, counts, gram, col_parts, target_mass, row_pot, x_norm, y_start, target_cells)
+    )(listed, gram, col_parts, target_mass, row_pot, x_norm, y_start, target_cells)
     packets = lax.all_to_all(packet, "t", 0, 0)
     quarters = call(mix_kernel, f32(SB, BLOCK, E), [], "mix", [VMEM])(packets)
     mapped = lax.all_to_all(quarters, "t", 0, 0)

time: 152 us -> 152 us (level)
  blocking collectives: 137 us -> 140 us
  Pallas kernels: 11.2 us -> 9.38 us
    all_to_all x3, blocking collectives: 24.9 us -> 26.6 us  [shards(): row_parts = lax.all_to_all(row_part, 't', 0, 0)]
where the time goes in v5:
time: 152 us
  blocking collectives  140 us (92%)
  Pallas kernels  9.38 us (6%)
    all_to_all x3, blocking collectives, shards(): col_parts = lax.all_to_all(col_part, 'z', 0, 0)  62.6 us
    all_to_all x3, blocking collectives, shards(): row_parts = lax.all_to_all(row_part, 't', 0, 0)  26.6 us
    all_to_all x3, blocking collectives, shards(): col_parts = lax.all_to_all(col_parts, ('x', 'c'), 0, 0)  26.3 us
    all_to_all x1, blocking collectives, shards(): packets = lax.all_to_all(packet, 't', 0, 0)  13.2 us
    all_to_all x1, blocking collectives, shards(): mapped = lax.all_to_all(quarters, 't', 0, 0)  10.8 us

profile of v5, /device:TPU:2, one launch (start us, length us, event | category | flops | bytes accessed | tf_op | source)
XLA Modules:
  0.0 151.7 jit_solution(15190098974362381879)
XLA Ops:
  0.6 0.0 copy-start
  0.6 0.0 copy-start.4
  0.7 0.0 copy-start.3
  0.7 0.0 copy-start.1
  0.7 0.0 copy-start.2
  1.4 0.4 copy-done
  1.9 0.0 copy-done.4
  1.9 0.0 copy-done.3
  1.9 0.1 copy-done.1
  1.9 2.4 %gram.1 = (f32[4,16,128,128]{3,2,1,0:T(8,128)S(1)}, f32[4,4,128]{2,1,0:T(4,128)S(1)}, f32[4,128]{1,0:T(4,128)S(1)}, f32[16,128]{1,0:T(8,128)S(1)}, f32[4,128]{1,0:T(4,128)S(1)}, /*index=5*/s32[8,128]{1,0:T(8,128)S(1)}) custom-call(s32[1,32]{1,0:T(1,128)S(1)} %bitcast.10, s32[1,1]{1,0:T(1,128)S(6)} %copy.10.counts, bf16[512,256]{1,0:T(8,128)(2,1)S(1)} %copy-done.1, ...), custom_call_target="tpu_custom_call" | custom-call | flops 1000000 | bytes 2000000 | tf_op jit(solution)/shard_map/gram/pallas_call | solution.py:397
  4.3 9.8 %all_to_all.55.partials = f32[4,4,128]{2,1,0:T(4,128)S(1)} all-to-all(f32[4,4,128]{2,1,0:T(4,128)S(1)} %get-tuple-element.24), channel_id=1, replica_groups=mesh['z'=16,'x'=4,'c'=2,'t'=4] {'t'}, dimensions={0} | all-to-all | bytes 16384 | tf_op jit(solution)/shard_map/all_to_all | solution.py:413
  14.1 1.5 cols.3
  15.6 28.7 %all_to_all.56.partials = f32[16,16,128]{2,1,0:T(8,128)S(1)} all-to-all(f32[16,16,128]{2,1,0:T(8,128)S(1)} %get-tuple-element.27), channel_id=1, replica_groups=mesh['z'=16,'x'=4,'c'=2,'t'=4] {'z'}, dimensions={0} | all-to-all | bytes 262144 | tf_op jit(solution)/shard_map/all_to_all | solution.py:421
  44.3 9.1 %all_to_all.57.partials = f32[8,16,128]{2,1,0:T(8,128)S(1)} all-to-all(f32[8,16,128]{2,1,0:T(8,128)S(1)} %merge.3), channel_id=1, replica_groups=mesh['z'=16,'x'=4,'c'=2,'t'=4] {'x','c'}, dimensions={0} | all-to-all | bytes 131072 | tf_op jit(solution)/shard_map/all_to_all | solution.py:423
  53.4 0.0 copy-done.2
  53.4 0.8 rows.2
  54.2 8.0 %all_to_all.58.partials = f32[4,4,128]{2,1,0:T(4,128)S(1)} all-to-all(f32[4,4,128]{2,1,0:T(4,128)S(1)} %get-tuple-element.29), channel_id=1, replica_groups=mesh['z'=16,'x'=4,'c'=2,'t'=4] {'t'}, dimensions={0} | all-to-all | bytes 16384 | tf_op jit(solution)/shard_map/all_to_all | solution.py:413
  62.2 0.7 cols.4
  62.9 17.0 %all_to_all.59.partials = f32[16,16,128]{2,1,0:T(8,128)S(1)} all-to-all(f32[16,16,128]{2,1,0:T(8,128)S(1)} %get-tuple-element.31), channel_id=1, replica_groups=mesh['z'=16,'x'=4,'c'=2,'t'=4] {'z'}, dimensions={0} | all-to-all | bytes 262144 | tf_op jit(solution)/shard_map/all_to_all | solution.py:421
  79.9 8.6 %all_to_all.60.partials = f32[8,16,128]{2,1,0:T(8,128)S(1)} all-to-all(f32[8,16,128]{2,1,0:T(8,128)S(1)} %merge.4), channel_id=1, replica_groups=mesh['z'=16,'x'=4,'c'=2,'t'=4] {'x','c'}, dimensions={0} | all-to-all | bytes 131072 | tf_op jit(solution)/shard_map/all_to_all | solution.py:423
  88.6 0.7 rows.3
  89.3 8.8 %all_to_all.61.partials = f32[4,4,128]{2,1,0:T(4,128)S(1)} all-to-all(f32[4,4,128]{2,1,0:T(4,128)S(1)} %get-tuple-element.33), channel_id=1, replica_groups=mesh['z'=16,'x'=4,'c'=2,'t'=4] {'t'}, dimensions={0} | all-to-all | bytes 16384 | tf_op jit(solution)/shard_map/all_to_all | solution.py:413
  98.1 0.7 cols.5
  98.8 16.8 %all_to_all.62.partials = f32[16,16,128]{2,1,0:T(8,128)S(1)} all-to-all(f32[16,16,128]{2,1,0:T(8,128)S(1)} %get-tuple-element.35), channel_id=1, replica_groups=mesh['z'=16,'x'=4,'c'=2,'t'=4] {'z'}, dimensions={0} | all-to-all | bytes 262144 | tf_op jit(solution)/shard_map/all_to_all | solution.py:421
  115.6 8.6 %all_to_all.63.partials = f32[8,16,128]{2,1,0:T(8,128)S(1)} all-to-all(f32[8,16,128]{2,1,0:T(8,128)S(1)} %merge.5), channel_id=1, replica_groups=mesh['z'=16,'x'=4,'c'=2,'t'=4] {'x','c'}, dimensions={0} | all-to-all | bytes 131072 | tf_op jit(solution)/shard_map/all_to_all | solution.py:423
  124.3 2.4 %mapping.1 = (f32[4,136,256]{2,1,0:T(8,128)S(1)}, f32[4,128]{1,0:T(4,128)}, f32[16,128]{1,0:T(8,128)}) custom-call(s32[8,128]{1,0:T(8,128)S(1)} %get-tuple-element.22.listed, f32[4,16,128,128]{3,2,1,0:T(8,128)S(1)} %get-tuple-element.23.gram, f32[8,16,128]{2,1,0:T(8,128)S(1)} %all_to_all.63.partials, f32[16,128]{1,0:T(8,128)S(1)} %bitcast.8, ...), custom_call_target="tpu_custom_call" | custom-call | flops 1000000 | bytes 2000000 | tf_op jit(solution)/shard_map/mapping/pallas_call | solution.py:432
  126.7 13.2 %all_to_all.64.packets = f32[4,136,256]{2,1,0:T(8,128)S(1)} all-to-all(f32[4,136,256]{2,1,0:T(8,128)S(1)} %get-tuple-element.40), channel_id=1, replica_groups=mesh['z'=16,'x'=4,'c'=2,'t'=4] {'t'}, dimensions={0} | all-to-all | bytes 1114112 | tf_op jit(solution)/shard_map/all_to_all | solution.py:440
  139.9 0.2 mix.1
  140.1 10.8 %all_to_all.65 = f32[4,128,256]{2,1,0:T(8,128)S(1)} all-to-all(f32[4,128,256]{2,1,0:T(8,128)S(1)} %mix.1), channel_id=1, replica_groups=mesh['z'=16,'x'=4,'c'=2,'t'=4] {'t'}, dimensions={0} | all-to-all | bytes 1048576 | tf_op jit(solution)/shard_map/all_to_all | solution.py:442
  150.9 0.8 copy.11
  (4 shorter events, 0.1 us)
Async XLA Ops:
  0.6 1.2 copy-start
  0.6 1.2 copy-start.4
  0.7 1.2 copy-start.3
  0.7 1.3 copy-start.1
  0.7 52.7 %copy-start.2 = (f32[2048]{0:T(1024)S(1)}, f32[2048]{0:T(1024)}, u32[]{:S(2)}) copy-start(f32[2048]{0:T(1024)} %param.9) | copy-start | bytes 24580

commit v6 on v5

--- a/solution.py
+++ b/solution.py
@@ -14,6 +14,9 @@
 E = 256
 XC = 8
 Z = 16
+LISTS = TB * BLOCK
+MASS = LISTS + 8
+HEIGHT = MASS + TB
 EPS = 0.02
 SRC = ("z", "x", "c")
 
@@ -21,6 +24,7 @@
 VMEM = pl.BlockSpec(memory_space=pltpu.VMEM)
 ANY = pl.BlockSpec(memory_space=pl.ANY)
 OFFSET = 70.0
+LIMIT = 51
 FIRST = 5000000000
 ROW_STEP = 4
 COL_STEP = 4
@@ -29,14 +33,14 @@
 FIRST_LIMIT = 52
 
 
-def call(kernel, out_shape, scratch, name, specs, out_specs=None, flops=1000000):
+def call(kernel, out_shape, scratch, name, specs, out_specs=None, flops=1000000, limit=16):
     return pl.pallas_call(
         kernel,
         out_shape=out_shape,
         in_specs=specs,
         out_specs=out_specs or jax.tree.map(lambda unused: VMEM, out_shape),
         scratch_shapes=scratch,
-        compiler_params=pltpu.CompilerParams(vmem_limit_bytes=16 * 1024 * 1024),
+        compiler_params=pltpu.CompilerParams(vmem_limit_bytes=limit * 1024 * 1024),
         cost_estimate=pl.CostEstimate(flops=flops, bytes_accessed=2000000, transcendentals=500000),
         name=name,
     )
@@ -106,7 +110,7 @@
     )
 
 
-def row_passes(pairs, live, gram, spread, peaks, sums, found, also):
+def row_passes(pairs, live, gram, spread, peaks, sums, found):
     peaks[...] = jnp.full(peaks.shape, -jnp.inf, jnp.float32)
     sums[...] = jnp.zeros(sums.shape, jnp.float32)
 
@@ -123,7 +127,6 @@
         p, q = entry(pairs, k)
         weight = jnp.exp(row_scores(gram, spread, p, q) - peaks[p])
         sums[p] += weight
-        also(p, q, weight)
         return unused
 
     lax.fori_loop(0, live, second, 0)
@@ -131,7 +134,7 @@
     found[...] = tops + jnp.log(row_totals(sums))
 
 
-def row_pass(pairs, live, gram, spread, before, row_spread, sums, found, peaks, also):
+def row_pass(pairs, live, gram, spread, before, row_spread, sums, found, peaks):
     sums[...] = jnp.zeros(sums.shape, jnp.float32)
 
     def only(slots):
@@ -139,7 +142,6 @@
         weights = [jnp.exp(row_scores(gram, spread, p, q) + row_spread[p]) for p, q in places]
         for (p, q), weight in zip(places, weights):
             sums[p] += weight
-            also(p, q, weight)
 
     each(live, ROW_STEP, only)
     logs = jnp.log(row_totals(sums))
@@ -147,7 +149,7 @@
 
     @pl.when(jnp.logical_not(in_range(logs)))
     def again():
-        row_passes(pairs, live, gram, spread, peaks, sums, found, also)
+        row_passes(pairs, live, gram, spread, peaks, sums, found)
 
 
 def folded(cells):
@@ -157,8 +159,15 @@
     return jnp.sum(square, axis=0, keepdims=True) * (1.0 / (E * EPS))
 
 
-def nothing(p, q, weight):
-    return None
+def multiplied(x, cells, c, gram):
+    dims = (((1,), (1,)), ((), ()))
+    crossed = lax.dot_general(x[...], cells, dims, preferred_element_type=jnp.float32)
+    crossed = crossed * (2.0 / (E * EPS))
+    for half in range(2):
+        for p in range(SB):
+            gram[p, 2 * c + half] = crossed[
+                p * BLOCK : (p + 1) * BLOCK, half * BLOCK : (half + 1) * BLOCK
+            ]
 
 
 def zero_kernel(zeros):
@@ -171,6 +180,7 @@
     x,
     y,
     mass,
+    y_mass,
     zeros,
     gram,
     partial,
@@ -178,7 +188,10 @@
     y_start,
     log_mass,
     listed,
+    wide_hbm,
     pairs,
+    wide,
+    done,
     spread,
     row_spread,
     peaks,
@@ -189,31 +202,42 @@
     listed[pl.ds(0, 1), pl.ds(0, MAXB)] = pairs_in[...]
     listed[pl.ds(1, 1), pl.ds(0, 1)] = counts[...]
     log_mass[...] = jnp.log(mass[...])
+    wide[pl.ds(LISTS, 8)] = jnp.zeros((8, E), jnp.float32)
+    wide[pl.ds(LISTS, 8), pl.ds(0, BLOCK)] = listed[...].astype(jnp.float32)
+    wide[pl.ds(MASS, TB)] = jnp.zeros((TB, E), jnp.float32)
+    wide[pl.ds(MASS, TB), pl.ds(0, BLOCK)] = y_mass[...]
+    copies = []
+
+    def send(start, size):
+        span = pl.ds(start, size)
+        copies.append(
+            pltpu.make_async_copy(wide.at[span], wide_hbm.at[span], done.at[len(copies)])
+        )
+        copies[-1].start()
+
+    send(LISTS, 8 + TB)
+    for c in range(TB // 4):
+        span = pl.ds(c * 4 * BLOCK, 4 * BLOCK)
+        wide[span] = y[span].astype(jnp.float32)
+        send(c * 4 * BLOCK, 4 * BLOCK)
     for p in range(SB):
         x_norm[pl.ds(p, 1)] = folded(x[pl.ds(p * BLOCK, BLOCK), :])
 
-    def chunk(c):
+    for c in range(TB // 2):
         cells = y[pl.ds(c * 2 * BLOCK, 2 * BLOCK), :]
-        dims = (((1,), (1,)), ((), ()))
-        crossed = lax.dot_general(x[...], cells, dims, preferred_element_type=jnp.float32)
-        crossed = crossed * (2.0 / (E * EPS))
+        multiplied(x, cells, c, gram)
         for half in range(2):
             norm = folded(cells[half * BLOCK : (half + 1) * BLOCK])
             spread[2 * c + half] = jnp.broadcast_to(-norm, (8, BLOCK))
-            for p in range(SB):
-                gram[p, 2 * c + half] = crossed[
-                    p * BLOCK : (p + 1) * BLOCK, half * BLOCK : (half + 1) * BLOCK
-                ]
-
-    for c in range(TB // 2):
-        chunk(c)
     y_start[...] = spread[...][:, 0]
     before = zeros[...] - x_norm[...]
     spread_rows(before + OFFSET, row_spread)
     live = fetch(listed, pairs)
-    row_pass(pairs, live, gram, spread, before, row_spread, sums, found, peaks, nothing)
+    row_pass(pairs, live, gram, spread, before, row_spread, sums, found, peaks)
     for d in range(SB):
         partial[d] = found[...]
+    for copy in copies:
+        copy.wait()
 
 
 def col_kernel(
@@ -300,7 +324,7 @@
     spread_rows(before[...] + OFFSET, row_spread)
     live = fetch(listed, pairs)
     row_pass(
-        pairs, live, gram, spread, before[...], row_spread, sums, found, peaks, nothing
+        pairs, live, gram, spread, before[...], row_spread, sums, found, peaks
     )
     for d in range(SB):
         partial[d] = found[...]
@@ -308,74 +332,148 @@
 
 def map_kernel(
     listed,
-    gram,
     partials,
     mass,
     before,
     x_norm,
     y_start,
+    x,
     y,
-    packet,
+    wide_hbm,
     row_pot,
     col_pot,
-    pairs,
+    mapped,
+    mask,
     done,
+    wide,
+    cells,
+    weights,
+    lists,
+    lse,
     spread,
     row_spread,
     peaks,
     sums,
-    found,
-    high,
-    low,
+    total,
     rows_out,
     cols_out,
 ):
-    potential = jnp.log(mass[...]) - log_sum(partials[...])
+    own = lax.axis_index("t")
+
+    def shard_of(i):
+        return (own + i) & (SB - 1)
+
+    def arrival(i):
+        rows = pl.ds(pl.multiple_of(shard_of(i) * HEIGHT, 8), HEIGHT)
+        return pltpu.make_async_copy(wide_hbm.at[rows], wide.at[i - 1], done.at[i - 1])
+
+    for i in range(1, SB):
+        arrival(i).start()
+    for t in range(SB):
+        lse[t] = log_sum(jnp.stack([partials[SB * k + t] for k in range(XC)]))
+    potential = jnp.log(mass[...]) - lse[own]
     rows_out[...] = EPS * (before[...] + x_norm[...])
     cols_out[...] = EPS * (potential - y_start[...])
     copies = [
-        pltpu.make_async_copy(rows_out, row_pot, done.at[0]),
-        pltpu.make_async_copy(cols_out, col_pot, done.at[1]),
+        pltpu.make_async_copy(rows_out, row_pot, done.at[SB - 1]),
+        pltpu.make_async_copy(cols_out, col_pot, done.at[SB]),
     ]
     for copy in copies:
         copy.start()
-    spread_cols(potential, spread)
     spread_rows(before[...] + OFFSET, row_spread)
-    high[...] = jnp.zeros(high.shape, jnp.bfloat16)
-    low[...] = jnp.zeros(low.shape, jnp.bfloat16)
-
-    def also(p, q, weight):
-        rows = pl.ds(pl.multiple_of(p * BLOCK, BLOCK), BLOCK)
-        cols = pl.ds(pl.multiple_of(q * BLOCK, BLOCK), BLOCK)
-        leading = weight.astype(jnp.bfloat16)
-        high[rows, cols] = leading
-        low[rows, cols] = (weight - leading.astype(jnp.float32)).astype(jnp.bfloat16)
-
-    live = fetch(listed, pairs)
-    row_pass(pairs, live, gram, spread, before[...], row_spread, sums, found, peaks, also)
-    total = jnp.dot(high[...], y[...], preferred_element_type=jnp.float32) + jnp.dot(
-        low[...], y[...], preferred_element_type=jnp.float32
-    )
+
+    def couple(found):
+        for k in range(SB * TB):
+            mask[k] = -jnp.inf
+        live = found[1, 0]
+        for k in range(MAXB):
+            mask[jnp.where(k < live, found[0, k], SB * TB)] = 0.0
+
+    def sweep(chunk_of, use):
+        dims = (((1,), (1,)), ((), ()))
+        for c in range(TB // 2):
+            crossed = lax.dot_general(x[...], chunk_of(c), dims, preferred_element_type=jnp.float32)
+            crossed = crossed * (2.0 / (E * EPS))
+            for p in range(SB):
+                for half in range(2):
+                    q = 2 * c + half
+                    part = crossed[p * BLOCK : (p + 1) * BLOCK, half * BLOCK : (half + 1) * BLOCK]
+                    part = part.reshape(BLOCK // 8, 8, BLOCK) + (spread[q] + mask[p * TB + q])[None]
+                    use(p, q, part.reshape(BLOCK, BLOCK))
+
+    def weigh(p, q, score):
+        weight = jnp.exp(score + row_spread[p]).astype(jnp.bfloat16)
+        weights[pl.ds(p * BLOCK, BLOCK), pl.ds(q * BLOCK, BLOCK)] = weight
+        sums[p] += weight.astype(jnp.float32)
+
+    def top(p, q, score):
+        peaks[p] = jnp.maximum(peaks[p], score)
+
+    def load_own():
+        spread_cols(jnp.log(mass[...]) - lse[own], spread)
+        couple(listed)
+
+    def own_chunk(c):
+        return y[pl.ds(c * 2 * BLOCK, 2 * BLOCK)]
+
+    def load(i):
+        other = wide.at[i - 1]
+        found = other[pl.ds(MASS, TB), pl.ds(0, BLOCK)]
+        spread_cols(jnp.log(found) - lse[shard_of(i)], spread)
+        lists[...] = other[pl.ds(LISTS, 8), pl.ds(0, BLOCK)].astype(jnp.int32)
+        couple(lists)
+
+    def chunk(i):
+        def of(c):
+            part = pl.ds(c * 2 * BLOCK, 2 * BLOCK)
+            narrow = wide[i - 1, part, :].astype(jnp.bfloat16)
+            cells[part] = narrow
+            return narrow
+
+        return of
+
+    def weigh_all(arrived):
+        sums[...] = jnp.zeros(sums.shape, jnp.float32)
+        load_own()
+        sweep(own_chunk, weigh)
+        total[...] = jnp.dot(weights[...], y[...], preferred_element_type=jnp.float32)
+
+        def other(i, unused):
+            if not arrived:
+                arrival(i).wait()
+            load(i)
+            sweep(chunk(i), weigh)
+            total[...] += jnp.dot(weights[...], cells[...], preferred_element_type=jnp.float32)
+            return unused
+
+        lax.fori_loop(1, SB, other, 0)
+
+    weigh_all(False)
+
+    @pl.when(jnp.logical_not(in_range(jnp.log(row_totals(sums)))))
+    def again():
+        peaks[...] = jnp.full(peaks.shape, -jnp.inf, jnp.float32)
+        load_own()
+        sweep(own_chunk, top)
+
+        def other(i, unused):
+            load(i)
+            sweep(chunk(i), top)
+            return unused
+
+        lax.fori_loop(1, SB, other, 0)
+        for p in range(SB):
+            highest = jnp.max(peaks[p], axis=1, keepdims=True)
+            row_spread[p] = jnp.broadcast_to(-highest, (BLOCK, BLOCK))
+        weigh_all(True)
+
     for p in range(SB):
-        packet[p, pl.ds(0, BLOCK), :] = total[p * BLOCK : (p + 1) * BLOCK] / jnp.sum(
-            sums[p], axis=1, keepdims=True
-        )
-        packet[p, pl.ds(BLOCK, 8), :] = jnp.concatenate(
-            [jnp.broadcast_to(found[pl.ds(p, 1)], (8, BLOCK))] * 2, axis=1
-        )
+        rows = pl.ds(p * BLOCK, BLOCK)
+        total[rows] = total[rows] / jnp.sum(sums[p], axis=1, keepdims=True)
+        copies.append(pltpu.make_async_copy(total.at[rows], mapped.at[rows], done.at[SB + 1 + p]))
+        copies[-1].start()
     for copy in copies:
         copy.wait()
-
-
-def mix_kernel(packets, mapped):
-    parts = jnp.concatenate([packets[t, pl.ds(BLOCK, 1), pl.ds(0, BLOCK)] for t in range(SB)])
-    share = jnp.exp(parts - jnp.max(parts, axis=0, keepdims=True))
-    share = share / jnp.sum(share, axis=0, keepdims=True)
-    total = jnp.zeros((BLOCK, E), jnp.float32)
-    for t in range(SB):
-        factor = turned(jnp.broadcast_to(share[t : t + 1], (BLOCK, BLOCK)))
-        total = total + jnp.concatenate([factor, factor], axis=1) * packets[t, pl.ds(0, BLOCK), :]
-    mapped[...] = jnp.broadcast_to(total[None], mapped.shape)
 
 
 def shards(source_cells, target_cells, source_mass, target_mass, pairs, counts):
@@ -387,14 +485,13 @@
     flat = pltpu.VMEM((TB, 8, BLOCK), jnp.float32)
     rows = pltpu.VMEM((SB, BLOCK), jnp.float32)
     cols = pltpu.VMEM((TB, BLOCK), jnp.float32)
-    dense = pltpu.VMEM((SB * BLOCK, TB * BLOCK), jnp.bfloat16)
     lists = [pltpu.SMEM((MAXB,), jnp.int32)]
 
     def sems(count):
         return pltpu.SemaphoreType.DMA((count,))
 
     zeros = call(zero_kernel, f32(SB, BLOCK), [], "zeros", [], flops=FIRST)()
-    gram, row_part, x_norm, y_start, source_log, listed = call(
+    gram, row_part, x_norm, y_start, source_log, listed, wide = call(
         gram_kernel,
         (
             f32(SB, TB, BLOCK, BLOCK),
@@ -403,11 +500,15 @@
             f32(TB, BLOCK),
             f32(SB, BLOCK),
             jax.ShapeDtypeStruct((8, BLOCK), jnp.int32),
+            f32(HEIGHT, E),
         ),
-        lists + [flat, tall, tall, tall, rows],
+        lists
+        + [pltpu.VMEM((HEIGHT, E), jnp.float32), sems(TB // 4 + 1), flat, tall, tall, tall, rows],
         "gram",
-        [VMEM] * 6,
-    )(pairs, counts, source_cells, target_cells, source_mass, zeros)
+        [VMEM] * 7,
+        out_specs=(VMEM,) * 6 + (ANY,),
+    )(pairs, counts, source_cells, target_cells, source_mass, target_mass, zeros)
+    wide = lax.all_gather(wide, "t", tiled=True)
     col_pot = y_start
     for iteration in range(ITERS):
         row_parts = lax.all_to_all(row_part, "t", 0, 0)
@@ -419,28 +520,53 @@
             [VMEM] + [VMEM] * 4,
         )(listed, gram, row_parts, source_log, col_pot)
         col_parts = lax.all_to_all(col_part, "z", 0, 0)
-        col_parts = call(merge_kernel, f32(XC, TB, BLOCK), [], "merge", [VMEM])(col_parts)
-        col_parts = lax.all_to_all(col_parts, ("x", "c"), 0, 0)
+        near = ("x", "c") if iteration < ITERS - 1 else ("x", "c", "t")
+        peers = XC if iteration < ITERS - 1 else XC * SB
+        col_parts = call(merge_kernel, f32(peers, TB, BLOCK), [], "merge", [VMEM])(col_parts)
+        col_parts = lax.all_to_all(col_parts, near, 0, 0)
         if iteration < ITERS - 1:
             row_part, col_pot = call(
                 row_kernel,
                 (f32(SB, SB, BLOCK), f32(TB, BLOCK)),
                 lists + [flat, tall, tall, tall, rows],
                 "rows",
-                [VMEM] + [VMEM] * 4,
+                [VMEM] * 5,
             )(listed, gram, col_parts, target_mass, row_pot)
-    packet, row_pot, col_pot = call(
+    row_pot, col_pot, mapped = call(
         map_kernel,
-        (f32(SB, BLOCK + 8, E), f32(SB, BLOCK), f32(TB, BLOCK)),
-        lists + [sems(2), flat, tall, tall, tall, rows, dense, dense, rows, cols],
+        (f32(SB, BLOCK), f32(TB, BLOCK), f32(SB * BLOCK, E)),
+        [
+            pltpu.SMEM((SB * TB + 1,), jnp.float32),
+            sems(2 * SB + 1),
+            pltpu.VMEM((SB - 1, HEIGHT, E), jnp.float32),
+            pltpu.VMEM((TB * BLOCK, E), jnp.bfloat16),
+            pltpu.VMEM((SB * BLOCK, TB * BLOCK), jnp.bfloat16),
+            pltpu.VMEM((8, BLOCK), jnp.int32),
+            pltpu.VMEM((SB, TB, BLOCK), jnp.float32),
+            flat,
+            tall,
+            tall,
+            tall,
+            pltpu.VMEM((SB * BLOCK, E), jnp.float32),
+            rows,
+            cols,
+        ],
         "mapping",
-        [VMEM] + [VMEM] * 7,
-        out_specs=(VMEM, ANY, ANY),
-    )(listed, gram, col_parts, target_mass, row_pot, x_norm, y_start, target_cells)
-    packets = lax.all_to_all(packet, "t", 0, 0)
-    quarters = call(mix_kernel, f32(SB, BLOCK, E), [], "mix", [VMEM])(packets)
-    mapped = lax.all_to_all(quarters, "t", 0, 0)
-    return row_pot.reshape(-1), col_pot.reshape(-1), mapped.reshape(SB * BLOCK, E)
+        [VMEM] * 8 + [ANY],
+        out_specs=(ANY, ANY, ANY),
+        limit=LIMIT,
+    )(
+        listed,
+        col_parts,
+        target_mass,
+        row_pot,
+        x_norm,
+        y_start,
+        source_cells,
+        target_cells,
+        wide,
+    )
+    return row_pot.reshape(-1), col_pot.reshape(-1), mapped
 
 
 def solution(mesh):

time: 152 us -> 158 us (1.039)
  the two profiles are of different devices: /device:TPU:2 before, /device:TPU:1 now
where the time goes in v6:
time: 158 us; the launch traced here: 157 us
  blocking collectives  121 us (77%)
  Pallas kernels  16.4 us (10%)
  between operations  14.9 us (9%)
  local copies, waits for them, and re-layouts  4.67 us (3%)
    all_to_all x3, blocking collectives, shards(): col_parts = lax.all_to_all(col_part, 'z', 0, 0)  56.4 us
    all_to_all x3, blocking collectives, shards(): col_parts = lax.all_to_all(col_parts, near, 0, 0)  41.5 us
    all_to_all x3, blocking collectives, shards(): row_parts = lax.all_to_all(row_part, 't', 0, 0)  23.5 us
    pallas_call x1, Pallas kernels, shards(): call(map_kernel, (f32(SB, BLOCK), f32(TB, BLOCK), f32(SB * BLOCK, E)), [p...  10.1 us
    unnamed x16, local copies, waits for them, and re-layouts  4.67 us
  transfers between devices with their start and end apart: 1, of which 0 were waited for; matrix products, arithmetic and copies ran while one was open for 0% of the time, Pallas kernels for 2%

profile of v6, /device:TPU:1, one launch (start us, length us, event | category | flops | bytes accessed | tf_op | source)
XLA Modules:
  0.0 157.5 jit_solution(11027980037784222229)
XLA Ops:
  7.2 0.0 copy-start.7
  7.2 0.0 copy-start.4
  7.2 0.0 copy-start.3
  7.2 0.0 copy-start.6
  7.2 0.0 copy-start.5
  7.2 0.0 all-gather.2.cloned.1.call-start
  8.0 0.0 copy-done.7
  8.0 0.1 copy-done.4
  8.1 0.4 copy-done.3
  8.5 0.0 copy-done.6
  8.5 0.0 copy-done.5
  8.5 2.6 %gram.1 = (f32[4,16,128,128]{3,2,1,0:T(8,128)S(1)}, f32[4,4,128]{2,1,0:T(4,128)S(1)}, f32[4,128]{1,0:T(4,128)S(1)}, f32[16,128]{1,0:T(8,128)S(1)}, f32[4,128]{1,...) custom-call(s32[1,32]{1,0:T(1,128)S(1)} %bitcast.10, s32[1,1]{1,0:T(1,128)S(6)} %copy.9.counts, ...), custom_call_target="tpu_custom_call" | custom-call | flops 1000000 | bytes 2000000 | tf_op jit(solution)/shard_map/gram/pallas_call | solution.py:494
  11.1 0.0 copy-start
  11.1 2.0 %copy-done = f32[4,16,128,128]{3,2,1,0:T(8,128)} copy-done((f32[4,16,128,128]{3,2,1,0:T(8,128)}, f32[4,16,128,128]{3,2,1,0:T(8,128)S(1)}, u32[]{:S(2)}) %copy-start) | copy-done | bytes 4194328
  13.1 0.0 all-gather.2.cloned.1.call-update
  13.1 9.5 %all_to_all.45.partials = f32[4,4,128]{2,1,0:T(4,128)S(1)} all-to-all(f32[4,4,128]{2,1,0:T(4,128)S(1)} %get-tuple-element.25), channel_id=1, replica_groups=mesh['z'=16,'x'=4,'c'=2,'t'=4] {'t'}, dimensions={0} | all-to-all | bytes 16384 | tf_op jit(solution)/shard_map/all_to_all | solution.py:514
  22.6 0.0 copy-start.1
  22.6 2.2 %copy-done.1 = f32[4,16,128,128]{3,2,1,0:T(8,128)S(1)} copy-done((f32[4,16,128,128]{3,2,1,0:T(8,128)S(1)}, f32[4,16,128,128]{3,2,1,0:T(8,128)}, u32[]{:S(2)}) %copy-start.1) | copy-done | bytes 4194328
  24.8 0.0 copy-start.2
  24.8 0.7 cols.3
  25.5 26.2 %all_to_all.46.partials = f32[16,16,128]{2,1,0:T(8,128)S(1)} all-to-all(f32[16,16,128]{2,1,0:T(8,128)S(1)} %get-tuple-element.28), channel_id=1, replica_groups=mesh['z'=16,'x'=4,'c'=2,'t'=4] {'z'}, dimensions={0} | all-to-all | bytes 262144 | tf_op jit(solution)/shard_map/all_to_all | solution.py:522
  51.8 13.3 %all_to_all.47.partials = f32[8,16,128]{2,1,0:T(8,128)S(1)} all-to-all(f32[8,16,128]{2,1,0:T(8,128)S(1)} %merge.3), channel_id=1, replica_groups=mesh['z'=16,'x'=4,'c'=2,'t'=4] {'x','c'}, dimensions={0} | all-to-all | bytes 131072 | tf_op jit(solution)/shard_map/all_to_all | solution.py:526
  65.1 0.0 copy-done.2
  65.1 0.8 rows.2
  65.9 7.2 %all_to_all.48.partials = f32[4,4,128]{2,1,0:T(4,128)S(1)} all-to-all(f32[4,4,128]{2,1,0:T(4,128)S(1)} %get-tuple-element.30), channel_id=1, replica_groups=mesh['z'=16,'x'=4,'c'=2,'t'=4] {'t'}, dimensions={0} | all-to-all | bytes 16384 | tf_op jit(solution)/shard_map/all_to_all | solution.py:514
  73.1 0.7 cols.4
  73.8 15.0 %all_to_all.49.partials = f32[16,16,128]{2,1,0:T(8,128)S(1)} all-to-all(f32[16,16,128]{2,1,0:T(8,128)S(1)} %get-tuple-element.32), channel_id=1, replica_groups=mesh['z'=16,'x'=4,'c'=2,'t'=4] {'z'}, dimensions={0} | all-to-all | bytes 262144 | tf_op jit(solution)/shard_map/all_to_all | solution.py:522
  88.9 11.5 %all_to_all.50.partials = f32[8,16,128]{2,1,0:T(8,128)S(1)} all-to-all(f32[8,16,128]{2,1,0:T(8,128)S(1)} %merge.4), channel_id=1, replica_groups=mesh['z'=16,'x'=4,'c'=2,'t'=4] {'x','c'}, dimensions={0} | all-to-all | bytes 131072 | tf_op jit(solution)/shard_map/all_to_all | solution.py:526
  100.4 0.8 rows.3
  101.2 6.7 %all_to_all.51.partials = f32[4,4,128]{2,1,0:T(4,128)S(1)} all-to-all(f32[4,4,128]{2,1,0:T(4,128)S(1)} %get-tuple-element.34), channel_id=1, replica_groups=mesh['z'=16,'x'=4,'c'=2,'t'=4] {'t'}, dimensions={0} | all-to-all | bytes 16384 | tf_op jit(solution)/shard_map/all_to_all | solution.py:514
  107.9 0.7 cols.5
  108.6 15.2 %all_to_all.52.partials = f32[16,16,128]{2,1,0:T(8,128)S(1)} all-to-all(f32[16,16,128]{2,1,0:T(8,128)S(1)} %get-tuple-element.36), channel_id=1, replica_groups=mesh['z'=16,'x'=4,'c'=2,'t'=4] {'z'}, dimensions={0} | all-to-all | bytes 262144 | tf_op jit(solution)/shard_map/all_to_all | solution.py:522
  123.8 0.1 merge.5
  123.9 16.6 %all_to_all.53.partials = f32[32,16,128]{2,1,0:T(8,128)S(1)} all-to-all(f32[32,16,128]{2,1,0:T(8,128)S(1)} %merge.5), channel_id=1, replica_groups=mesh['z'=16,'x'=4,'c'=2,'t'=4] {'x','c','t'}, dimensions={0} | all-to-all | bytes 524288 | tf_op jit(solution)/shard_map/all_to_all | solution.py:526
  140.5 0.0 all-gather.2.cloned.1.call-done.wide_hbm
  140.5 10.1 %mapping.1 = (f32[4,128]{1,0:T(4,128)}, f32[16,128]{1,0:T(8,128)}, f32[512,256]{1,0:T(8,128)}) custom-call(s32[8,128]{1,0:T(8,128)S(1)} %get-tuple-element.23.listed, f32[32,16,128]{2,1,0:T(8,128)S(1)} %all_to_all.53.partials, f32[16,128]{1,0:T(8,128)S(1)} %bitcast.8, f32[4,128]{1,0:T(4,128)S(1)} %get-tuple-element.37.before, ...), custom_call_target="tpu_custom_call" | custom-call | flops 1000000 | bytes 2000000 | tf_op jit(solution)/shard_map/mapping/pallas_call | solution.py:535
  (3 shorter events, 0.1 us)
Async XLA Ops:
  7.2 0.8 copy-start.7
  7.2 1.0 copy-start.4
  7.2 1.3 copy-start.3
  7.2 1.3 copy-start.6
  7.2 1.3 copy-start.5
  7.2 133.3 %all-gather.2.cloned.1.call-start = ((), (), s32[]{:S(2)}) async-start(), calls=%async_computation.9 | async-start | bytes 10608640 | tf_op jit(solution)/shard_map/all_gather | solution.py:511
  11.1 2.0 %copy-start = (f32[4,16,128,128]{3,2,1,0:T(8,128)}, f32[4,16,128,128]{3,2,1,0:T(8,128)S(1)}, u32[]{:S(2)}) copy-start(f32[4,16,128,128]{3,2,1,0:T(8,128)S(1)} %get-tuple-element.24.gram) | copy-start | bytes 12582916
  22.6 2.2 %copy-start.1 = (f32[4,16,128,128]{3,2,1,0:T(8,128)S(1)}, f32[4,16,128,128]{3,2,1,0:T(8,128)}, u32[]{:S(2)}) copy-start(f32[4,16,128,128]{3,2,1,0:T(8,128)} %copy-done) | copy-start | bytes 12582916
  24.8 40.3 %copy-start.2 = (f32[4,16,128,128]{3,2,1,0:T(8,128)S(1)}, f32[4,16,128,128]{3,2,1,0:T(8,128)}, u32[]{:S(2)}) copy-start(f32[4,16,128,128]{3,2,1,0:T(8,128)} %copy-done) | copy-start | bytes 12582916
Sparse Core Ops, SparseCore 0:
  13.2 97.2 all-gather.1

commit v7 on v5

--- a/solution.py
+++ b/solution.py
@@ -22,8 +22,8 @@
 ANY = pl.BlockSpec(memory_space=pl.ANY)
 OFFSET = 70.0
 FIRST = 5000000000
-ROW_STEP = 4
-COL_STEP = 4
+STEP = 4
+BITS = 6
 MIDDLE = 10.0
 REACH = 74.0
 FIRST_LIMIT = 52
@@ -47,29 +47,44 @@
 
 
 def fetch(listed, pairs):
-    for k in range(MAXB):
+    for k in range(MAXB // STEP):
         pairs[k] = listed[0, k]
-    return listed[1, 0]
-
-
-def each(live, step, body):
-    whole = live >> (step.bit_length() - 1)
+    return listed[0, MAXB // STEP]
+
+
+def packed(pairs_in, counts):
+    lane = lax.broadcasted_iota(jnp.int32, (8, BLOCK), 1)
+    words = jnp.where(lane == MAXB // STEP, counts[0, 0], 0)
+    for k in range(MAXB // STEP):
+        word = pairs_in[0, k * STEP]
+        for j in range(1, STEP):
+            word = word | (pairs_in[0, k * STEP + j] << (BITS * j))
+        words = jnp.where(lane == k, word, words)
+    return words
+
+
+def each(live, body):
+    whole = live >> 2
 
     def several(i, unused):
-        body([i * step + j for j in range(step)])
+        body([(i, j) for j in range(STEP)])
         return unused
 
     def single(k, unused):
-        body([k])
+        body([(whole, k - whole * STEP)])
         return unused
 
     lax.fori_loop(0, whole, several, 0)
-    lax.fori_loop(whole * step, live, single, 0)
+    lax.fori_loop(whole * STEP, live, single, 0)
+
+
+def place(pairs, slot):
+    value = pairs[slot[0]] >> (BITS * slot[1])
+    return (value >> 4) & 3, value & 15
 
 
 def entry(pairs, k):
-    value = pairs[k]
-    return value >> 4, value & 15
+    return place(pairs, (k >> 2, k & 3))
 
 
 def turned(block):
@@ -135,13 +150,13 @@
     sums[...] = jnp.zeros(sums.shape, jnp.float32)
 
     def only(slots):
-        places = [entry(pairs, k) for k in slots]
+        places = [place(pairs, slot) for slot in slots]
         weights = [jnp.exp(row_scores(gram, spread, p, q) + row_spread[p]) for p, q in places]
         for (p, q), weight in zip(places, weights):
             sums[p] += weight
             also(p, q, weight)
 
-    each(live, ROW_STEP, only)
+    each(live, only)
     logs = jnp.log(row_totals(sums))
     found[...] = logs - (before + OFFSET)
 
@@ -185,9 +200,7 @@
     sums,
     found,
 ):
-    listed[...] = jnp.zeros(listed.shape, jnp.int32)
-    listed[pl.ds(0, 1), pl.ds(0, MAXB)] = pairs_in[...]
-    listed[pl.ds(1, 1), pl.ds(0, 1)] = counts[...]
+    listed[...] = packed(pairs_in, counts)
     log_mass[...] = jnp.log(mass[...])
     for p in range(SB):
         x_norm[pl.ds(p, 1)] = folded(x[pl.ds(p * BLOCK, BLOCK), :])
@@ -224,16 +237,16 @@
     before,
     partial,
     potential,
+    spread,
     pairs,
-    spread,
     col_spread,
     peaks,
     sums,
     found,
 ):
     potential[...] = mass_log[...] - log_sum(partials[...])
-    spread_rows(potential[...], spread)
-    spread_cols(before[...] + OFFSET, col_spread)
+    spread_rows(potential[...] + OFFSET, spread)
+    spread_cols(before[...], col_spread)
     sums[...] = jnp.zeros(sums.shape, jnp.float32)
     live = fetch(listed, pairs)
 
@@ -241,12 +254,12 @@
         return (spread[p] + gram[p, q]).reshape(BLOCK // 8, 8, BLOCK)
 
     def only(slots):
-        places = [entry(pairs, k) for k in slots]
+        places = [place(pairs, slot) for slot in slots]
         parts = [jnp.sum(jnp.exp(scores(p, q) + col_spread[q][None]), axis=0) for p, q in places]
         for (p, q), part in zip(places, parts):
             sums[q] += part
 
-    each(live, COL_STEP, only)
+    each(live, only)
     logs = jnp.log(jnp.sum(sums[...], axis=1))
     found[...] = logs - (before[...] + OFFSET)
 
@@ -269,7 +282,7 @@
             return unused
 
         lax.fori_loop(0, live, second, 0)
-        found[...] = peaks[...][:, 0] + jnp.log(jnp.sum(sums[...], axis=1))
+        found[...] = peaks[...][:, 0] - OFFSET + jnp.log(jnp.sum(sums[...], axis=1))
 
     for d in range(Z):
         partial[d] = found[...]
@@ -286,18 +299,17 @@
     partials,
     mass,
     before,
+    row_spread,
     partial,
     potential,
     pairs,
     spread,
-    row_spread,
     peaks,
     sums,
     found,
 ):
     potential[...] = jnp.log(mass[...]) - log_sum(partials[...])
     spread_cols(potential[...], spread)
-    spread_rows(before[...] + OFFSET, row_spread)
     live = fetch(listed, pairs)
     row_pass(
         pairs, live, gram, spread, before[...], row_spread, sums, found, peaks, nothing
@@ -312,6 +324,7 @@
     partials,
     mass,
     before,
+    row_spread,
     x_norm,
     y_start,
     y,
@@ -321,7 +334,6 @@
     pairs,
     done,
     spread,
-    row_spread,
     peaks,
     sums,
     found,
@@ -340,7 +352,6 @@
     for copy in copies:
         copy.start()
     spread_cols(potential, spread)
-    spread_rows(before[...] + OFFSET, row_spread)
     high[...] = jnp.zeros(high.shape, jnp.bfloat16)
     low[...] = jnp.zeros(low.shape, jnp.bfloat16)
 
@@ -388,7 +399,7 @@
     rows = pltpu.VMEM((SB, BLOCK), jnp.float32)
     cols = pltpu.VMEM((TB, BLOCK), jnp.float32)
     dense = pltpu.VMEM((SB * BLOCK, TB * BLOCK), jnp.bfloat16)
-    lists = [pltpu.SMEM((MAXB,), jnp.int32)]
+    lists = [pltpu.SMEM((MAXB // STEP,), jnp.int32)]
 
     def sems(count):
         return pltpu.SemaphoreType.DMA((count,))
@@ -411,12 +422,12 @@
     col_pot = y_start
     for iteration in range(ITERS):
         row_parts = lax.all_to_all(row_part, "t", 0, 0)
-        col_part, row_pot = call(
+        col_part, row_pot, row_spread = call(
             col_kernel,
-            (f32(Z, TB, BLOCK), f32(SB, BLOCK)),
-            lists + [tall, flat, flat, flat, cols],
+            (f32(Z, TB, BLOCK), f32(SB, BLOCK), f32(SB, BLOCK, BLOCK)),
+            lists + [flat, flat, flat, cols],
             "cols",
-            [VMEM] + [VMEM] * 4,
+            [VMEM] * 5,
         )(listed, gram, row_parts, source_log, col_pot)
         col_parts = lax.all_to_all(col_part, "z", 0, 0)
         col_parts = call(merge_kernel, f32(XC, TB, BLOCK), [], "merge", [VMEM])(col_parts)
@@ -425,18 +436,18 @@
             row_part, col_pot = call(
                 row_kernel,
                 (f32(SB, SB, BLOCK), f32(TB, BLOCK)),
-                lists + [flat, tall, tall, tall, rows],
+                lists + [flat, tall, tall, rows],
                 "rows",
-                [VMEM] + [VMEM] * 4,
-            )(listed, gram, col_parts, target_mass, row_pot)
+                [VMEM] * 6,
+            )(listed, gram, col_parts, target_mass, row_pot, row_spread)
     packet, row_pot, col_pot = call(
         map_kernel,
         (f32(SB, BLOCK + 8, E), f32(SB, BLOCK), f32(TB, BLOCK)),
-        lists + [sems(2), flat, tall, tall, tall, rows, dense, dense, rows, cols],
+        lists + [sems(2), flat, tall, tall, rows, dense, dense, rows, cols],
         "mapping",
-        [VMEM] + [VMEM] * 7,
+        [VMEM] * 9,
         out_specs=(VMEM, ANY, ANY),
-    )(listed, gram, col_parts, target_mass, row_pot, x_norm, y_start, target_cells)
+    )(listed, gram, col_parts, target_mass, row_pot, row_spread, x_norm, y_start, target_cells)
     packets = lax.all_to_all(packet, "t", 0, 0)
     quarters = call(mix_kernel, f32(SB, BLOCK, E), [], "mix", [VMEM])(packets)
     mapped = lax.all_to_all(quarters, "t", 0, 0)

time: 152 us -> 152 us (level)
  no operation moved by 1% of the time
where the time goes in v7:
time: 152 us; the launch traced here: 151 us
  blocking collectives  139 us (91%)
  Pallas kernels  9.03 us (6%)
    all_to_all x3, blocking collectives, shards(): col_parts = lax.all_to_all(col_part, 'z', 0, 0)  62.8 us
    all_to_all x3, blocking collectives, shards(): row_parts = lax.all_to_all(row_part, 't', 0, 0)  27.1 us
    all_to_all x3, blocking collectives, shards(): col_parts = lax.all_to_all(col_parts, ('x', 'c'), 0, 0)  24.9 us
    all_to_all x1, blocking collectives, shards(): packets = lax.all_to_all(packet, 't', 0, 0)  13.4 us
    all_to_all x1, blocking collectives, shards(): mapped = lax.all_to_all(quarters, 't', 0, 0)  11.2 us

profile of v7, /device:TPU:2, one launch (start us, length us, event | category | flops | bytes accessed | tf_op | source)
XLA Modules:
  0.0 151.2 jit_solution(6023114709792772724)
XLA Ops:
  0.6 0.0 copy-start
  0.6 0.0 copy-start.4
  0.7 0.0 copy-start.3
  0.7 0.0 copy-start.1
  0.7 0.0 copy-start.2
  1.4 0.4 copy-done
  1.9 0.0 copy-done.4
  1.9 0.0 copy-done.3
  1.9 0.1 copy-done.1
  1.9 2.7 %gram.1 = (f32[4,16,128,128]{3,2,1,0:T(8,128)S(1)}, f32[4,4,128]{2,1,0:T(4,128)S(1)}, f32[4,128]{1,0:T(4,128)S(1)}, f32[16,128]{1,0:T(8,128)S(1)}, f32[4,128]{1,0:T(4,128)S(1)}, /*index=5*/s32[8,128]{1,0:T(8,128)S(1)}) custom-call(s32[1,32]{1,0:T(1,128)S(1)} %bitcast.10, s32[1,1]{1,0:T(1,128)S(6)} %copy.10.counts, bf16[512,256]{1,0:T(8,128)(2,1)S(1)} %copy-done.1, ...), custom_call_target="tpu_custom_call" | custom-call | flops 1000000 | bytes 2000000 | tf_op jit(solution)/shard_map/gram/pallas_call | solution.py:408
  4.6 9.4 %all_to_all.55.partials = f32[4,4,128]{2,1,0:T(4,128)S(1)} all-to-all(f32[4,4,128]{2,1,0:T(4,128)S(1)} %get-tuple-element.27), channel_id=1, replica_groups=mesh['z'=16,'x'=4,'c'=2,'t'=4] {'t'}, dimensions={0} | all-to-all | bytes 16384 | tf_op jit(solution)/shard_map/all_to_all | solution.py:424
  14.1 0.7 cols.3
  14.8 28.8 %all_to_all.56.partials = f32[16,16,128]{2,1,0:T(8,128)S(1)} all-to-all(f32[16,16,128]{2,1,0:T(8,128)S(1)} %get-tuple-element.30), channel_id=1, replica_groups=mesh['z'=16,'x'=4,'c'=2,'t'=4] {'z'}, dimensions={0} | all-to-all | bytes 262144 | tf_op jit(solution)/shard_map/all_to_all | solution.py:432
  43.6 8.9 %all_to_all.57.partials = f32[8,16,128]{2,1,0:T(8,128)S(1)} all-to-all(f32[8,16,128]{2,1,0:T(8,128)S(1)} %merge.3), channel_id=1, replica_groups=mesh['z'=16,'x'=4,'c'=2,'t'=4] {'x','c'}, dimensions={0} | all-to-all | bytes 131072 | tf_op jit(solution)/shard_map/all_to_all | solution.py:434
  52.6 0.0 copy-done.2
  52.6 0.7 rows.2
  53.3 9.0 %all_to_all.58.partials = f32[4,4,128]{2,1,0:T(4,128)S(1)} all-to-all(f32[4,4,128]{2,1,0:T(4,128)S(1)} %get-tuple-element.33), channel_id=1, replica_groups=mesh['z'=16,'x'=4,'c'=2,'t'=4] {'t'}, dimensions={0} | all-to-all | bytes 16384 | tf_op jit(solution)/shard_map/all_to_all | solution.py:424
  62.3 0.7 cols.4
  63.0 17.2 %all_to_all.59.partials = f32[16,16,128]{2,1,0:T(8,128)S(1)} all-to-all(f32[16,16,128]{2,1,0:T(8,128)S(1)} %get-tuple-element.35), channel_id=1, replica_groups=mesh['z'=16,'x'=4,'c'=2,'t'=4] {'z'}, dimensions={0} | all-to-all | bytes 262144 | tf_op jit(solution)/shard_map/all_to_all | solution.py:432
  80.2 7.9 %all_to_all.60.partials = f32[8,16,128]{2,1,0:T(8,128)S(1)} all-to-all(f32[8,16,128]{2,1,0:T(8,128)S(1)} %merge.4), channel_id=1, replica_groups=mesh['z'=16,'x'=4,'c'=2,'t'=4] {'x','c'}, dimensions={0} | all-to-all | bytes 131072 | tf_op jit(solution)/shard_map/all_to_all | solution.py:434
  88.1 0.7 rows.3
  88.9 8.7 %all_to_all.61.partials = f32[4,4,128]{2,1,0:T(4,128)S(1)} all-to-all(f32[4,4,128]{2,1,0:T(4,128)S(1)} %get-tuple-element.38), channel_id=1, replica_groups=mesh['z'=16,'x'=4,'c'=2,'t'=4] {'t'}, dimensions={0} | all-to-all | bytes 16384 | tf_op jit(solution)/shard_map/all_to_all | solution.py:424
  97.6 0.7 cols.5
  98.3 16.8 %all_to_all.62.partials = f32[16,16,128]{2,1,0:T(8,128)S(1)} all-to-all(f32[16,16,128]{2,1,0:T(8,128)S(1)} %get-tuple-element.40), channel_id=1, replica_groups=mesh['z'=16,'x'=4,'c'=2,'t'=4] {'z'}, dimensions={0} | all-to-all | bytes 262144 | tf_op jit(solution)/shard_map/all_to_all | solution.py:432
  115.1 8.0 %all_to_all.63.partials = f32[8,16,128]{2,1,0:T(8,128)S(1)} all-to-all(f32[8,16,128]{2,1,0:T(8,128)S(1)} %merge.5), channel_id=1, replica_groups=mesh['z'=16,'x'=4,'c'=2,'t'=4] {'x','c'}, dimensions={0} | all-to-all | bytes 131072 | tf_op jit(solution)/shard_map/all_to_all | solution.py:434
  123.1 2.5 %mapping.1 = (f32[4,136,256]{2,1,0:T(8,128)S(1)}, f32[4,128]{1,0:T(4,128)}, f32[16,128]{1,0:T(8,128)}) custom-call(s32[8,128]{1,0:T(8,128)S(1)} %get-tuple-element.25.listed, f32[4,16,128,128]{3,2,1,0:T(8,128)S(1)} %get-tuple-element.26.gram, f32[8,16,128]{2,1,0:T(8,128)S(1)} %all_to_all.63.partials, f32[16,128]{1,0:T(8,128)S(1)} %bitcast.8, ...), custom_call_target="tpu_custom_call" | custom-call | flops 1000000 | bytes 2000000 | tf_op jit(solution)/shard_map/mapping/pallas_call | solution.py:443
  125.6 13.4 %all_to_all.64.packets = f32[4,136,256]{2,1,0:T(8,128)S(1)} all-to-all(f32[4,136,256]{2,1,0:T(8,128)S(1)} %get-tuple-element.46), channel_id=1, replica_groups=mesh['z'=16,'x'=4,'c'=2,'t'=4] {'t'}, dimensions={0} | all-to-all | bytes 1114112 | tf_op jit(solution)/shard_map/all_to_all | solution.py:451
  139.0 0.2 mix.1
  139.2 11.2 %all_to_all.65 = f32[4,128,256]{2,1,0:T(8,128)S(1)} all-to-all(f32[4,128,256]{2,1,0:T(8,128)S(1)} %mix.1), channel_id=1, replica_groups=mesh['z'=16,'x'=4,'c'=2,'t'=4] {'t'}, dimensions={0} | all-to-all | bytes 1048576 | tf_op jit(solution)/shard_map/all_to_all | solution.py:453
  150.4 0.8 copy.11
  (4 shorter events, 0.1 us)
Async XLA Ops:
  0.6 1.2 copy-start
  0.6 1.2 copy-start.4
  0.7 1.2 copy-start.3
  0.7 1.3 copy-start.1
  0.7 51.9 %copy-start.2 = (f32[2048]{0:T(1024)S(1)}, f32[2048]{0:T(1024)}, u32[]{:S(2)}) copy-start(f32[2048]{0:T(1024)} %param.9) | copy-start | bytes 24580

commit v8 on v7

--- a/solution.py
+++ b/solution.py
@@ -284,7 +284,7 @@
         lax.fori_loop(0, live, second, 0)
         found[...] = peaks[...][:, 0] - OFFSET + jnp.log(jnp.sum(sums[...], axis=1))
 
-    for d in range(Z):
+    for d in range(partial.shape[0]):
         partial[d] = found[...]
 
 
@@ -421,17 +421,20 @@
     )(pairs, counts, source_cells, target_cells, source_mass, zeros)
     col_pot = y_start
     for iteration in range(ITERS):
+        far, near = ("z", Z), (("x", "c"), XC)
+        first, second = (far, near) if iteration < ITERS - 1 else (near, far)
         row_parts = lax.all_to_all(row_part, "t", 0, 0)
         col_part, row_pot, row_spread = call(
             col_kernel,
-            (f32(Z, TB, BLOCK), f32(SB, BLOCK), f32(SB, BLOCK, BLOCK)),
+            (f32(first[1], TB, BLOCK), f32(SB, BLOCK), f32(SB, BLOCK, BLOCK)),
             lists + [flat, flat, flat, cols],
             "cols",
             [VMEM] * 5,
         )(listed, gram, row_parts, source_log, col_pot)
-        col_parts = lax.all_to_all(col_part, "z", 0, 0)
-        col_parts = call(merge_kernel, f32(XC, TB, BLOCK), [], "merge", [VMEM])(col_parts)
-        col_parts = lax.all_to_all(col_parts, ("x", "c"), 0, 0)
+        col_parts = lax.all_to_all(col_part, first[0], 0, 0)
+        merged = f32(second[1], TB, BLOCK)
+        col_parts = call(merge_kernel, merged, [], "merge", [VMEM])(col_parts)
+        col_parts = lax.all_to_all(col_parts, second[0], 0, 0)
         if iteration < ITERS - 1:
             row_part, col_pot = call(
                 row_kernel,

time: 152 us -> 149 us (0.980)
  the two profiles are of different devices: /device:TPU:2 before, /device:TPU:32 now
where the time goes in v8:
time: 149 us
  blocking collectives  137 us (92%)
  Pallas kernels  9.95 us (7%)
  between operations  1.49 us (1%)
    all_to_all x3, blocking collectives, shards(): col_parts = lax.all_to_all(col_part, first[0], 0, 0)  52.1 us
    all_to_all x3, blocking collectives, shards(): col_parts = lax.all_to_all(col_parts, second[0], 0, 0)  36.2 us
    all_to_all x3, blocking collectives, shards(): row_parts = lax.all_to_all(row_part, 't', 0, 0)  27.1 us
    all_to_all x1, blocking collectives, shards(): packets = lax.all_to_all(packet, 't', 0, 0)  10.7 us
    all_to_all x1, blocking collectives, shards(): mapped = lax.all_to_all(quarters, 't', 0, 0)  10.5 us
    pallas_call x1, Pallas kernels, shards(): call(gram_kernel, (f32(SB, TB, BLOCK, BLOCK), f32(SB, SB, BLOCK), f32(SB,...  2.99 us

profile of v8, /device:TPU:32, one launch (start us, length us, event | category | flops | bytes accessed | tf_op | source)
XLA Modules:
  0.0 149.3 jit_solution(12139825052898232482)
XLA Ops:
  0.6 0.0 copy-start
  0.6 0.0 copy-start.4
  0.7 0.0 copy-start.3
  0.7 0.0 copy-start.1
  0.7 0.0 copy-start.2
  1.4 0.4 copy-done
  1.9 0.0 copy-done.4
  1.9 0.0 copy-done.3
  1.9 0.1 copy-done.1
  1.9 3.0 %gram.1 = (f32[4,16,128,128]{3,2,1,0:T(8,128)S(1)}, f32[4,4,128]{2,1,0:T(4,128)S(1)}, f32[4,128]{1,0:T(4,128)S(1)}, f32[16,128]{1,0:T(8,128)S(1)}, f32[4,128]{1,0:T(4,128)S(1)}, /*index=5*/s32[8,128]{1,0:T(8,128)S(1)}) custom-call(s32[1,32]{1,0:T(1,128)S(1)} %bitcast.10, s32[1,1]{1,0:T(1,128)S(6)} %copy.10.counts, bf16[512,256]{1,0:T(8,128)(2,1)S(1)} %copy-done.1, ...), custom_call_target="tpu_custom_call" | custom-call | flops 1000000 | bytes 2000000 | tf_op jit(solution)/shard_map/gram/pallas_call | solution.py:408
  4.9 9.3 %all_to_all.55.partials = f32[4,4,128]{2,1,0:T(4,128)S(1)} all-to-all(f32[4,4,128]{2,1,0:T(4,128)S(1)} %get-tuple-element.27), channel_id=1, replica_groups=mesh['z'=16,'x'=4,'c'=2,'t'=4] {'t'}, dimensions={0} | all-to-all | bytes 16384 | tf_op jit(solution)/shard_map/all_to_all | solution.py:426
  14.2 0.8 cols.3
  15.0 27.2 %all_to_all.56.partials = f32[16,16,128]{2,1,0:T(8,128)S(1)} all-to-all(f32[16,16,128]{2,1,0:T(8,128)S(1)} %get-tuple-element.30), channel_id=1, replica_groups=mesh['z'=16,'x'=4,'c'=2,'t'=4] {'z'}, dimensions={0} | all-to-all | bytes 262144 | tf_op jit(solution)/shard_map/all_to_all | solution.py:434
  42.2 10.1 %all_to_all.57.partials = f32[8,16,128]{2,1,0:T(8,128)S(1)} all-to-all(f32[8,16,128]{2,1,0:T(8,128)S(1)} %merge.3), channel_id=1, replica_groups=mesh['z'=16,'x'=4,'c'=2,'t'=4] {'x','c'}, dimensions={0} | all-to-all | bytes 131072 | tf_op jit(solution)/shard_map/all_to_all | solution.py:437
  52.4 0.0 copy-done.2
  52.4 0.8 rows.2
  53.2 8.9 %all_to_all.58.partials = f32[4,4,128]{2,1,0:T(4,128)S(1)} all-to-all(f32[4,4,128]{2,1,0:T(4,128)S(1)} %get-tuple-element.33), channel_id=1, replica_groups=mesh['z'=16,'x'=4,'c'=2,'t'=4] {'t'}, dimensions={0} | all-to-all | bytes 16384 | tf_op jit(solution)/shard_map/all_to_all | solution.py:426
  62.1 0.8 cols.4
  62.9 16.9 %all_to_all.59.partials = f32[16,16,128]{2,1,0:T(8,128)S(1)} all-to-all(f32[16,16,128]{2,1,0:T(8,128)S(1)} %get-tuple-element.35), channel_id=1, replica_groups=mesh['z'=16,'x'=4,'c'=2,'t'=4] {'z'}, dimensions={0} | all-to-all | bytes 262144 | tf_op jit(solution)/shard_map/all_to_all | solution.py:434
  79.8 8.0 %all_to_all.60.partials = f32[8,16,128]{2,1,0:T(8,128)S(1)} all-to-all(f32[8,16,128]{2,1,0:T(8,128)S(1)} %merge.4), channel_id=1, replica_groups=mesh['z'=16,'x'=4,'c'=2,'t'=4] {'x','c'}, dimensions={0} | all-to-all | bytes 131072 | tf_op jit(solution)/shard_map/all_to_all | solution.py:437
  87.8 0.8 rows.3
  88.6 8.9 %all_to_all.61.partials = f32[4,4,128]{2,1,0:T(4,128)S(1)} all-to-all(f32[4,4,128]{2,1,0:T(4,128)S(1)} %get-tuple-element.38), channel_id=1, replica_groups=mesh['z'=16,'x'=4,'c'=2,'t'=4] {'t'}, dimensions={0} | all-to-all | bytes 16384 | tf_op jit(solution)/shard_map/all_to_all | solution.py:426
  97.6 0.8 cols.5
  98.3 8.0 %all_to_all.62.partials = f32[8,16,128]{2,1,0:T(8,128)S(1)} all-to-all(f32[8,16,128]{2,1,0:T(8,128)S(1)} %get-tuple-element.40), channel_id=1, replica_groups=mesh['z'=16,'x'=4,'c'=2,'t'=4] {'x','c'}, dimensions={0} | all-to-all | bytes 131072 | tf_op jit(solution)/shard_map/all_to_all | solution.py:434
  106.4 18.1 %all_to_all.63.partials = f32[16,16,128]{2,1,0:T(8,128)S(1)} all-to-all(f32[16,16,128]{2,1,0:T(8,128)S(1)} %merge.5), channel_id=1, replica_groups=mesh['z'=16,'x'=4,'c'=2,'t'=4] {'z'}, dimensions={0} | all-to-all | bytes 262144 | tf_op jit(solution)/shard_map/all_to_all | solution.py:437
  124.5 2.7 %mapping.1 = (f32[4,136,256]{2,1,0:T(8,128)S(1)}, f32[4,128]{1,0:T(4,128)}, f32[16,128]{1,0:T(8,128)}) custom-call(s32[8,128]{1,0:T(8,128)S(1)} %get-tuple-element.25.listed, f32[4,16,128,128]{3,2,1,0:T(8,128)S(1)} %get-tuple-element.26.gram, f32[16,16,128]{2,1,0:T(8,128)S(1)} %all_to_all.63.partials, f32[16,128]{1,0:T(8,128)S(1)} %bitcast.8, ...), custom_call_target="tpu_custom_call" | custom-call | flops 1000000 | bytes 2000000 | tf_op jit(solution)/shard_map/mapping/pallas_call | solution.py:446
  127.2 10.7 %all_to_all.64.packets = f32[4,136,256]{2,1,0:T(8,128)S(1)} all-to-all(f32[4,136,256]{2,1,0:T(8,128)S(1)} %get-tuple-element.46), channel_id=1, replica_groups=mesh['z'=16,'x'=4,'c'=2,'t'=4] {'t'}, dimensions={0} | all-to-all | bytes 1114112 | tf_op jit(solution)/shard_map/all_to_all | solution.py:454
  137.8 0.2 mix.1
  138.0 10.5 %all_to_all.65 = f32[4,128,256]{2,1,0:T(8,128)S(1)} all-to-all(f32[4,128,256]{2,1,0:T(8,128)S(1)} %mix.1), channel_id=1, replica_groups=mesh['z'=16,'x'=4,'c'=2,'t'=4] {'t'}, dimensions={0} | all-to-all | bytes 1048576 | tf_op jit(solution)/shard_map/all_to_all | solution.py:456
  148.5 0.8 copy.11
  (4 shorter events, 0.1 us)
Async XLA Ops:
  0.6 1.2 copy-start
  0.6 1.2 copy-start.4
  0.7 1.2 copy-start.3
  0.7 1.3 copy-start.1
  0.7 51.7 %copy-start.2 = (f32[2048]{0:T(1024)S(1)}, f32[2048]{0:T(1024)}, u32[]{:S(2)}) copy-start(f32[2048]{0:T(1024)} %param.9) | copy-start | bytes 24580

commit v9 on v8

--- a/solution.py
+++ b/solution.py
@@ -422,7 +422,7 @@
     col_pot = y_start
     for iteration in range(ITERS):
         far, near = ("z", Z), (("x", "c"), XC)
-        first, second = (far, near) if iteration < ITERS - 1 else (near, far)
+        first, second = (far, near) if 0 < iteration < ITERS - 1 else (near, far)
         row_parts = lax.all_to_all(row_part, "t", 0, 0)
         col_part, row_pot, row_spread = call(
             col_kernel,

time: 149 us -> 152 us (1.020)
  Pallas kernels: 9.95 us -> 12 us
    all_to_all x3, blocking collectives: 36.2 us -> 55.4 us  [shards(): col_parts = lax.all_to_all(col_parts, second[0], 0, 0)]
    all_to_all x3, blocking collectives: 52.1 us -> 35.3 us  [shards(): col_parts = lax.all_to_all(col_part, first[0], 0, 0)]
    pallas_call x3, Pallas kernels: 2.32 us -> 5.15 us  [shards(): call(col_kernel, (f32(first[1], TB, BLOCK), f32(SB, BLOCK), f32(SB, BLOCK...]
    all_to_all x3, blocking collectives: 27.1 us -> 25.1 us  [shards(): row_parts = lax.all_to_all(row_part, 't', 0, 0)]
where the time goes in v9:
time: 152 us
  blocking collectives  137 us (90%)
  Pallas kernels  12 us (8%)
    all_to_all x3, blocking collectives, shards(): col_parts = lax.all_to_all(col_parts, second[0], 0, 0)  55.4 us
    all_to_all x3, blocking collectives, shards(): col_parts = lax.all_to_all(col_part, first[0], 0, 0)  35.3 us
    all_to_all x3, blocking collectives, shards(): row_parts = lax.all_to_all(row_part, 't', 0, 0)  25.1 us
    all_to_all x1, blocking collectives, shards(): packets = lax.all_to_all(packet, 't', 0, 0)  10.6 us
    all_to_all x1, blocking collectives, shards(): mapped = lax.all_to_all(quarters, 't', 0, 0)  10.5 us
    pallas_call x3, Pallas kernels, shards(): call(col_kernel, (f32(first[1], TB, BLOCK), f32(SB, BLOCK), f32(SB, BLOCK...  5.15 us

profile of v9, /device:TPU:32, one launch (start us, length us, event | category | flops | bytes accessed | tf_op | source)
XLA Modules:
  0.0 151.7 jit_solution(12537203905863954691)
XLA Ops:
  0.6 0.0 copy-start
  0.6 0.0 copy-start.4
  0.7 0.0 copy-start.3
  0.7 0.0 copy-start.1
  0.7 0.0 copy-start.2
  1.4 0.4 copy-done
  1.9 0.0 copy-done.4
  1.9 0.0 copy-done.3
  1.9 0.1 copy-done.1
  1.9 2.6 %gram.1 = (f32[4,16,128,128]{3,2,1,0:T(8,128)S(1)}, f32[4,4,128]{2,1,0:T(4,128)S(1)}, f32[4,128]{1,0:T(4,128)S(1)}, f32[16,128]{1,0:T(8,128)S(1)}, f32[4,128]{1,0:T(4,128)S(1)}, /*index=5*/s32[8,128]{1,0:T(8,128)S(1)}) custom-call(s32[1,32]{1,0:T(1,128)S(1)} %bitcast.10, s32[1,1]{1,0:T(1,128)S(6)} %copy.10.counts, bf16[512,256]{1,0:T(8,128)(2,1)S(1)} %copy-done.1, ...), custom_call_target="tpu_custom_call" | custom-call | flops 1000000 | bytes 2000000 | tf_op jit(solution)/shard_map/gram/pallas_call | solution.py:408
  4.6 9.6 %all_to_all.55.partials = f32[4,4,128]{2,1,0:T(4,128)S(1)} all-to-all(f32[4,4,128]{2,1,0:T(4,128)S(1)} %get-tuple-element.27), channel_id=1, replica_groups=mesh['z'=16,'x'=4,'c'=2,'t'=4] {'t'}, dimensions={0} | all-to-all | bytes 16384 | tf_op jit(solution)/shard_map/all_to_all | solution.py:426
  14.2 1.7 %cols.3 = (f32[8,16,128]{2,1,0:T(8,128)S(1)}, f32[4,128]{1,0:T(4,128)S(1)}, f32[4,128,128]{2,1,0:T(8,128)S(1)}) custom-call(s32[8,128]{1,0:T(8,128)S(1)} %get-tuple-element.25.listed, f32[4,16,128,128]{3,2,1,0:T(8,128)S(1)} %get-tuple-element.26.gram, f32[4,4,128]{2,1,0:T(4,128)S(1)} %all_to_all.55.partials, f32[4,128]{1,0:T(4,128)S(1)} %get-tuple-element.28.mass_log, ...), custom_call_target="tpu_custom_call" | custom-call | flops 1000000 | bytes 2000000 | tf_op jit(solution)/shard_map/cols/pallas_call | solution.py:427
  15.9 9.9 %all_to_all.56.partials = f32[8,16,128]{2,1,0:T(8,128)S(1)} all-to-all(f32[8,16,128]{2,1,0:T(8,128)S(1)} %get-tuple-element.30), channel_id=1, replica_groups=mesh['z'=16,'x'=4,'c'=2,'t'=4] {'x','c'}, dimensions={0} | all-to-all | bytes 131072 | tf_op jit(solution)/shard_map/all_to_all | solution.py:434
  25.8 28.6 %all_to_all.57.partials = f32[16,16,128]{2,1,0:T(8,128)S(1)} all-to-all(f32[16,16,128]{2,1,0:T(8,128)S(1)} %merge.3), channel_id=1, replica_groups=mesh['z'=16,'x'=4,'c'=2,'t'=4] {'z'}, dimensions={0} | all-to-all | bytes 262144 | tf_op jit(solution)/shard_map/all_to_all | solution.py:437
  54.5 0.0 copy-done.2
  54.5 0.7 rows.2
  55.2 7.9 %all_to_all.58.partials = f32[4,4,128]{2,1,0:T(4,128)S(1)} all-to-all(f32[4,4,128]{2,1,0:T(4,128)S(1)} %get-tuple-element.33), channel_id=1, replica_groups=mesh['z'=16,'x'=4,'c'=2,'t'=4] {'t'}, dimensions={0} | all-to-all | bytes 16384 | tf_op jit(solution)/shard_map/all_to_all | solution.py:426
  63.1 1.7 %cols.4 = (f32[16,16,128]{2,1,0:T(8,128)S(1)}, f32[4,128]{1,0:T(4,128)S(1)}, f32[4,128,128]{2,1,0:T(8,128)S(1)}) custom-call(s32[8,128]{1,0:T(8,128)S(1)} %get-tuple-element.25.listed, f32[4,16,128,128]{3,2,1,0:T(8,128)S(1)} %get-tuple-element.26.gram, f32[4,4,128]{2,1,0:T(4,128)S(1)} %all_to_all.58.partials, f32[4,128]{1,0:T(4,128)S(1)} %get-tuple-element.28.mass_log, ...), custom_call_target="tpu_custom_call" | custom-call | flops 1000000 | bytes 2000000 | tf_op jit(solution)/shard_map/cols/pallas_call | solution.py:427
  64.8 17.4 %all_to_all.59.partials = f32[16,16,128]{2,1,0:T(8,128)S(1)} all-to-all(f32[16,16,128]{2,1,0:T(8,128)S(1)} %get-tuple-element.35), channel_id=1, replica_groups=mesh['z'=16,'x'=4,'c'=2,'t'=4] {'z'}, dimensions={0} | all-to-all | bytes 262144 | tf_op jit(solution)/shard_map/all_to_all | solution.py:434
  82.3 8.0 %all_to_all.60.partials = f32[8,16,128]{2,1,0:T(8,128)S(1)} all-to-all(f32[8,16,128]{2,1,0:T(8,128)S(1)} %merge.4), channel_id=1, replica_groups=mesh['z'=16,'x'=4,'c'=2,'t'=4] {'x','c'}, dimensions={0} | all-to-all | bytes 131072 | tf_op jit(solution)/shard_map/all_to_all | solution.py:437
  90.3 0.7 rows.3
  91.0 7.7 %all_to_all.61.partials = f32[4,4,128]{2,1,0:T(4,128)S(1)} all-to-all(f32[4,4,128]{2,1,0:T(4,128)S(1)} %get-tuple-element.38), channel_id=1, replica_groups=mesh['z'=16,'x'=4,'c'=2,'t'=4] {'t'}, dimensions={0} | all-to-all | bytes 16384 | tf_op jit(solution)/shard_map/all_to_all | solution.py:426
  98.6 1.7 %cols.5 = (f32[8,16,128]{2,1,0:T(8,128)S(1)}, f32[4,128]{1,0:T(4,128)S(1)}, f32[4,128,128]{2,1,0:T(8,128)S(1)}) custom-call(s32[8,128]{1,0:T(8,128)S(1)} %get-tuple-element.25.listed, f32[4,16,128,128]{3,2,1,0:T(8,128)S(1)} %get-tuple-element.26.gram, f32[4,4,128]{2,1,0:T(4,128)S(1)} %all_to_all.61.partials, f32[4,128]{1,0:T(4,128)S(1)} %get-tuple-element.28.mass_log, ...), custom_call_target="tpu_custom_call" | custom-call | flops 1000000 | bytes 2000000 | tf_op jit(solution)/shard_map/cols/pallas_call | solution.py:427
  100.3 8.0 %all_to_all.62.partials = f32[8,16,128]{2,1,0:T(8,128)S(1)} all-to-all(f32[8,16,128]{2,1,0:T(8,128)S(1)} %get-tuple-element.40), channel_id=1, replica_groups=mesh['z'=16,'x'=4,'c'=2,'t'=4] {'x','c'}, dimensions={0} | all-to-all | bytes 131072 | tf_op jit(solution)/shard_map/all_to_all | solution.py:434
  108.4 18.7 %all_to_all.63.partials = f32[16,16,128]{2,1,0:T(8,128)S(1)} all-to-all(f32[16,16,128]{2,1,0:T(8,128)S(1)} %merge.5), channel_id=1, replica_groups=mesh['z'=16,'x'=4,'c'=2,'t'=4] {'z'}, dimensions={0} | all-to-all | bytes 262144 | tf_op jit(solution)/shard_map/all_to_all | solution.py:437
  127.1 2.5 %mapping.1 = (f32[4,136,256]{2,1,0:T(8,128)S(1)}, f32[4,128]{1,0:T(4,128)}, f32[16,128]{1,0:T(8,128)}) custom-call(s32[8,128]{1,0:T(8,128)S(1)} %get-tuple-element.25.listed, f32[4,16,128,128]{3,2,1,0:T(8,128)S(1)} %get-tuple-element.26.gram, f32[16,16,128]{2,1,0:T(8,128)S(1)} %all_to_all.63.partials, f32[16,128]{1,0:T(8,128)S(1)} %bitcast.8, ...), custom_call_target="tpu_custom_call" | custom-call | flops 1000000 | bytes 2000000 | tf_op jit(solution)/shard_map/mapping/pallas_call | solution.py:446
  129.6 10.6 %all_to_all.64.packets = f32[4,136,256]{2,1,0:T(8,128)S(1)} all-to-all(f32[4,136,256]{2,1,0:T(8,128)S(1)} %get-tuple-element.46), channel_id=1, replica_groups=mesh['z'=16,'x'=4,'c'=2,'t'=4] {'t'}, dimensions={0} | all-to-all | bytes 1114112 | tf_op jit(solution)/shard_map/all_to_all | solution.py:454
  140.3 0.2 mix.1
  140.5 10.5 %all_to_all.65 = f32[4,128,256]{2,1,0:T(8,128)S(1)} all-to-all(f32[4,128,256]{2,1,0:T(8,128)S(1)} %mix.1), channel_id=1, replica_groups=mesh['z'=16,'x'=4,'c'=2,'t'=4] {'t'}, dimensions={0} | all-to-all | bytes 1048576 | tf_op jit(solution)/shard_map/all_to_all | solution.py:456
  150.9 0.8 copy.11
  (4 shorter events, 0.1 us)
Async XLA Ops:
  0.6 1.2 copy-start
  0.6 1.2 copy-start.4
  0.7 1.2 copy-start.3
  0.7 1.3 copy-start.1
  0.7 53.8 %copy-start.2 = (f32[2048]{0:T(1024)S(1)}, f32[2048]{0:T(1024)}, u32[]{:S(2)}) copy-start(f32[2048]{0:T(1024)} %param.9) | copy-start | bytes 24580
